TPU v7x, 128 devices: a whole 4x4x4 slice. The times are simulated.
128 devices in a mesh: shard: 16 (over z, x_lo, core), ctx: 8 (over x_hi, y).
Axes of the slice: x: 4 (x_hi: 2, x_lo: 2; x = x_hi * 2 + x_lo), y: 4, z: 4, core: 2. Of those that a mesh axis runs over, the one named last changes fastest.
Arguments:
- hidden_in: bfloat16 [32, 1024, 1024], P('shard', 'ctx'), may hold values from -6 to 6
- routes: int32 [32, 1024, 8], P('shard', 'ctx'), may hold values from 0 to 31, all different within a row; in each aligned block of 128 rows (0 to 127, 128 to 255, ..., all dimensions but the last counted through in order) at most 48 rows name the same one
- prefix: int32 [32], P('shard'), may hold values from 102 to 512
- gain_attention: bfloat16 [1024], P('shard'), may hold values from 0.5 to 1.5
- w_query: bfloat16 [1024, 1024], P('shard'), may hold values from -0.1875 to 0.1875
- w_keyval: bfloat16 [1024, 1024], P('shard'), may hold values from -0.1875 to 0.1875
- gain_query: bfloat16 [1024], P('shard'), may hold values from 0.5 to 1.5
- gain_key: bfloat16 [512], P('shard'), may hold values from 0.5 to 1.5
- w_output: bfloat16 [1024, 1024], P('shard'), may hold values from -3 to 3
- gain_experts: bfloat16 [1024], P('shard'), may hold values from 0.5 to 1.5
- w_router: bfloat16 [1024, 32], P('shard'), may hold values from -0.09375 to 0.09375
- w_gate_up: bfloat16 [32, 1024, 1024], P('shard', 'ctx'), may hold values from -0.1875 to 0.1875
- w_down: bfloat16 [32, 512, 1024], P('shard', None, 'ctx'), may hold values from -1 to 1
- cotangent: bfloat16 [32, 1024, 1024], P('shard', 'ctx'), may hold values from -6 to 6
Outputs:
- layer_out: bfloat16 [32, 1024, 1024], P('shard', 'ctx')
- grad_input: bfloat16 [32, 1024, 1024], P('shard', 'ctx')
- grad_gain_attention: float32 [1024], P('shard')
- query_weight_gradient: float32 [1024, 1024], P('shard')
- grad_w_keyval: float32 [1024, 1024], P('shard')
- grad_gain_query: float32 [1024], P('shard')
- grad_gain_key: float32 [512], P('shard')
- grad_w_output: float32 [1024, 1024], P('shard')
- grad_gain_experts: float32 [1024], P('shard')
- grad_w_router: float32 [1024, 32], P('shard')
- grad_w_gate_up: float32 [32, 1024, 1024], P('shard', 'ctx')
- grad_w_down: float32 [32, 512, 1024], P('shard', None, 'ctx')
Inputs may be any that keep to these rules, and one draw needn't show every extreme that they name: `routes`: in each aligned block of 128 positions of a sequence, at most 48 tokens name one expert; a token names 8 different experts.
All inputs are finite; a program needn't handle non-finite values.
Results may differ from a plain program's by a relative error of at most 0.028.
Values may be sent and summed in bfloat16 or wider, within the bound.
No kernel may reach another device: no remote copies, remote signals or barrier semaphores. Data moves between devices by JAX's collectives and lax.ppermute only.
A program may use at most 256 MiB of HBM per device.

v0:
```python
import math

import jax
import jax.numpy as jnp
from jax import lax
from jax.sharding import PartitionSpec as P

H = 16
KVH = 8
HD = 64
FF = 512
E = 32
TOPK = 8
SEQ_LEN = 1024


EPSILON = 1e-06
ROPE_BASE = 10000.0
MASKED = -1e30


def sent_together(arrays, axis, dim, along):
    widths = [math.prod(a.shape[along:]) for a in arrays]
    both = jnp.concatenate(
        [a.reshape(*a.shape[:along], w) for a, w in zip(arrays, widths)], axis=along
    )
    result = lax.all_gather(both, axis, axis=dim, tiled=True)
    pieces = jnp.split(result, [sum(widths[:k]) for k in range(1, len(widths))], axis=along)
    return tuple(
        (b.reshape(*result.shape[:along], *a.shape[along:]) for a, b in zip(arrays, pieces))
    )


def gather_turned(arrays, axis, dims):
    turned = [jnp.moveaxis(a, dim, 0) for a, dim in zip(arrays, dims)]
    widths = [t[0].size for t in turned]
    both = jnp.concatenate([t.reshape(-1, w) for t, w in zip(turned, widths)], axis=1)
    result = lax.all_gather(both, axis, axis=0, tiled=True)
    pieces = jnp.split(result, [sum(widths[:k]) for k in range(1, len(widths))], axis=1)
    return tuple(
        (
            jnp.moveaxis(b.reshape(-1, *t.shape[1:]), 0, dim)
            for b, t, dim in zip(pieces, turned, dims)
        )
    )


def side_by_side(arrays, axis, dim, along):
    widths = [a.shape[along] for a in arrays]
    both = jnp.concatenate(arrays, axis=along)
    result = lax.all_gather(both, axis, axis=dim, tiled=True)
    return tuple(jnp.split(result, [sum(widths[:k]) for k in range(1, len(widths))], axis=along))


def side_by_side_2(arrays, axis, dim, along):
    both = jnp.concatenate(arrays, axis=along)
    result, at, finished = (lax.psum_scatter(both, axis, scatter_dimension=dim, tiled=True), 0, [])
    for a in arrays:
        finished.append(lax.slice_in_dim(result, at, at + a.shape[along], axis=along))
        at += a.shape[along]
    return tuple(finished)


def side_by_side_3(arrays, axis, dim, along):
    widths = [math.prod(a.shape[along:]) for a in arrays]
    both = jnp.concatenate(
        [a.reshape(*a.shape[:along], w) for a, w in zip(arrays, widths)], axis=along
    )
    result = lax.psum_scatter(both, axis, scatter_dimension=dim, tiled=True)
    pieces = jnp.split(result, [sum(widths[:k]) for k in range(1, len(widths))], axis=along)
    return tuple(
        (b.reshape(*result.shape[:along], *a.shape[along:]) for a, b in zip(arrays, pieces))
    )


def copy_for_each(array, axis):
    count = lax.axis_size(axis)
    return lax.all_to_all(
        jnp.broadcast_to(array[None], (count, *array.shape)), axis, 0, 0, tiled=True
    )


def of_everyone(array, axis):
    return copy_for_each(array, axis).astype(jnp.float32).sum(axis=0)


def split_up(array, dim, count):
    before, after = (array.shape[:dim], array.shape[dim + 1 :])
    return jnp.moveaxis(array.reshape(*before, count, -1, *after), dim, 0)


def one_scatter(arrays, axis, dims):
    count = lax.axis_size(axis)
    pieces = [split_up(a, dim, count) for a, dim in zip(arrays, dims)]
    lines = jnp.concatenate([b.reshape(count, -1) for b in pieces], axis=1)
    rows = max(16, -(-lines.shape[1] // 1024) * 8)
    lines = jnp.pad(lines, ((0, 0), (0, rows * 128 - lines.shape[1]))).reshape(-1, 128)
    vector, at, finished = (lax.psum_scatter(lines, axis, tiled=True).reshape(-1), 0, [])
    for b in pieces:
        part = b[0]
        finished.append(vector[at : at + part.size].reshape(part.shape))
        at += part.size
    return tuple(finished)


def slot_tables(route_rows, block_len, capacity):
    blocks = route_rows.reshape(-1, block_len * TOPK)
    block_count = blocks.shape[0]
    onehot = (blocks[:, :, None] == jnp.arange(E, dtype=jnp.int32)).astype(jnp.int32)
    slot_index = jnp.sum((jnp.cumsum(onehot, axis=1) - 1) * onehot, axis=2)
    block_base = jnp.arange(block_count, dtype=jnp.int32)[:, None] * capacity
    entry_slot = (blocks * (block_count * capacity) + block_base + slot_index).reshape(-1)
    entry_count = entry_slot.shape[0]
    entries = jnp.arange(entry_count, dtype=jnp.int32)
    slot_table = (
        jnp.full((E * block_count * capacity,), entry_count, jnp.int32).at[entry_slot].set(entries)
    )
    return (slot_table.reshape(E, block_count * capacity), entry_slot)


def rope_tables(positions):
    half_dim = HD // 2
    frequency = ROPE_BASE ** (-2.0 * jnp.arange(half_dim, dtype=jnp.float32) / HD)
    angles = positions.astype(jnp.float32)[:, None] * frequency[None, :]
    return (jnp.cos(angles), jnp.sin(angles))


def apply_spin_phase(heads_in, cosine, sine_table):
    half_dim = HD // 2
    lower_half = heads_in[..., :half_dim]
    upper_half = heads_in[..., half_dim:]
    cos_part = cosine[:, None, :]
    sin_part = sine_table[:, None, :]
    return jnp.concatenate(
        [
            lower_half * cos_part - upper_half * sin_part,
            upper_half * cos_part + lower_half * sin_part,
        ],
        axis=-1,
    )


def rotate_back(grad_heads, cosine, sine_table):
    half_dim = HD // 2
    lower_half = grad_heads[..., :half_dim]
    upper_half = grad_heads[..., half_dim:]
    cos_part = cosine[:, None, :]
    sin_part = sine_table[:, None, :]
    return jnp.concatenate(
        [
            lower_half * cos_part + upper_half * sin_part,
            upper_half * cos_part - lower_half * sin_part,
        ],
        axis=-1,
    )


def inverse_scale(content_vectors_entering):
    return lax.rsqrt(
        jnp.mean(content_vectors_entering * content_vectors_entering, axis=-1, keepdims=True)
        + EPSILON
    )


def norm_back(content_vectors_entering, factor, gain_vec, grad_norm):
    weighted = grad_norm * gain_vec
    row_inner = jnp.mean(weighted * content_vectors_entering, axis=-1, keepdims=True)
    grad_values = (
        factor * weighted - content_vectors_entering * factor * factor * factor * row_inner
    )
    gain_grad = jnp.sum(
        (grad_norm * content_vectors_entering * factor).reshape(
            -1, content_vectors_entering.shape[-1]
        ),
        axis=0,
    )
    return (grad_values, gain_grad)


def local(
    hidden_in,
    routes,
    prefix,
    gain_attention,
    w_query,
    w_keyval,
    gain_query,
    gain_key,
    w_output,
    gain_experts,
    w_router,
    w_gate_up,
    w_down,
    cotangent,
):
    dense = (
        *sent_together((gain_attention, w_query, w_keyval, gain_query), "shard", 0, 1),
        lax.all_gather(gain_key, "shard", axis=0, tiled=True),
        *sent_together((w_output, gain_experts, w_router), "shard", 0, 1),
    )
    (
        full_gain_one,
        complete_query_proj,
        complete_keyval_proj,
        full_gain_query,
        full_gain_key,
        entire_head_merge_map,
        full_gain_two,
        full_router,
    ) = dense
    expert_gate_up, expert_down = gather_turned((w_gate_up, w_down), "ctx", (1, 2))
    seq_count, block_len, model_width = hidden_in.shape
    kv_width = complete_keyval_proj.shape[1] // 2
    group_size = H // KVH
    token_count = seq_count * block_len
    capacity = block_len * 3 // 8
    shard_count = lax.axis_size("shard")
    offset = lax.axis_index("ctx") * block_len
    positions = offset + jnp.arange(block_len, dtype=jnp.int32)
    cosine, sine_table = rope_tables(positions)
    lookup_location = jnp.arange(SEQ_LEN, dtype=jnp.int32)
    visible = (lookup_location[None, None, :] <= positions[None, :, None]) | (
        lookup_location[None, None, :] < prefix[:, None, None]
    )
    visible = visible[:, None, None, :, :]
    layer_inputs = hidden_in.astype(jnp.float32)
    first_gain = full_gain_one.astype(jnp.float32)
    scale_one = inverse_scale(layer_inputs)
    normalized_rows = (layer_inputs * scale_one * first_gain).astype(jnp.bfloat16)
    query_rows = jnp.einsum(
        "owv,vz->owz", normalized_rows, complete_query_proj, preferred_element_type=jnp.float32
    )
    keyval_rows = jnp.einsum(
        "owv,vz->owz", normalized_rows, complete_keyval_proj, preferred_element_type=jnp.float32
    )
    keys_raw = keyval_rows[..., :kv_width]
    values_own = keyval_rows[..., kv_width:].astype(jnp.bfloat16)
    query_gain = full_gain_query.astype(jnp.float32)
    key_gain = full_gain_key.astype(jnp.float32)
    scale_query = inverse_scale(query_rows)
    scale_key = inverse_scale(keys_raw)
    query_rot = apply_spin_phase(
        (query_rows * scale_query * query_gain).reshape(seq_count, block_len, H, HD),
        cosine,
        sine_table,
    ).astype(jnp.bfloat16)
    key_rot = apply_spin_phase(
        (keys_raw * scale_key * key_gain).reshape(seq_count, block_len, KVH, HD), cosine, sine_table
    ).astype(jnp.bfloat16)
    keys_all, values_all = side_by_side(
        (key_rot.reshape(seq_count, block_len, kv_width), values_own), "ctx", 1, 0
    )
    keys_all = keys_all.reshape(seq_count, SEQ_LEN, KVH, HD)
    values_all = values_all.reshape(seq_count, SEQ_LEN, KVH, HD)
    query_groups = query_rot.reshape(seq_count, block_len, KVH, group_size, HD)

    def score_block():
        raw_scores = jnp.einsum(
            "sqkgd,slkd->skgql", query_groups, keys_all, preferred_element_type=jnp.float32
        ) * HD ** (-0.5)
        return jnp.where(visible, raw_scores, MASKED)

    scores = score_block()
    row_peak = jnp.max(scores, axis=-1, keepdims=True)
    log_total = row_peak + jnp.log(jnp.sum(jnp.exp(scores - row_peak), axis=-1, keepdims=True))
    weights_low = jnp.exp(scores - log_total).astype(jnp.bfloat16)
    attention_result = jnp.einsum(
        "skgql,slkd->sqkgd", weights_low, values_all, preferred_element_type=jnp.float32
    )
    attention_result = attention_result.reshape(seq_count, block_len, model_width).astype(
        jnp.bfloat16
    )
    residual_stream = layer_inputs + jnp.einsum(
        "owv,vz->owz", attention_result, entire_head_merge_map, preferred_element_type=jnp.float32
    )
    second_gain = full_gain_two.astype(jnp.float32)
    scale_two = inverse_scale(residual_stream)
    expert_in = (
        (residual_stream * scale_two * second_gain)
        .astype(jnp.bfloat16)
        .reshape(token_count, model_width)
    )
    logits = jnp.dot(expert_in, full_router, preferred_element_type=jnp.float32)
    route_rows = routes.reshape(token_count, TOPK)
    picked = route_rows[:, :, None] == jnp.arange(E, dtype=jnp.int32)
    chosen = jnp.sum(jnp.where(picked, logits[:, None, :], 0.0), axis=-1)
    gate_probs = jax.nn.softmax(chosen, axis=-1)
    slot_table, entry_slot = slot_tables(route_rows, block_len, capacity)
    padded_rows = jnp.concatenate([expert_in, jnp.zeros((1, model_width), jnp.bfloat16)])
    outgoing = padded_rows[slot_table // TOPK].reshape(
        shard_count, E // shard_count, -1, model_width
    )
    arrived = lax.all_to_all(outgoing, "shard", split_axis=0, concat_axis=0, tiled=True)
    gate_up = jnp.einsum(
        "nerd,edf->nerf", arrived, expert_gate_up, preferred_element_type=jnp.float32
    )
    gate_part = gate_up[..., :FF]
    up_part = gate_up[..., FF:]
    gate_sigmoid = jax.nn.sigmoid(gate_part)
    middle = (gate_part * gate_sigmoid * up_part).astype(jnp.bfloat16)
    expert_out = jnp.einsum(
        "nerf,efd->nerd", middle, expert_down, preferred_element_type=jnp.float32
    ).astype(jnp.bfloat16)
    returned = lax.all_to_all(expert_out, "shard", split_axis=0, concat_axis=0, tiled=True).reshape(
        -1, model_width
    )
    per_entry = returned[entry_slot].reshape(token_count, TOPK, model_width).astype(jnp.float32)
    mixed_out = residual_stream.reshape(token_count, model_width) + jnp.sum(
        gate_probs[:, :, None] * per_entry, axis=1
    )
    layer_out = mixed_out.reshape(seq_count, block_len, model_width).astype(jnp.bfloat16)
    grad_out = cotangent.astype(jnp.float32).reshape(token_count, model_width)
    grad_gate = jnp.sum(grad_out[:, None, :] * per_entry, axis=-1)
    grad_chosen = gate_probs * (grad_gate - jnp.sum(gate_probs * grad_gate, axis=-1, keepdims=True))
    grad_logits = jnp.sum(jnp.where(picked, grad_chosen[:, :, None], 0.0), axis=1).astype(
        jnp.bfloat16
    )
    grad_entries = (
        (gate_probs[:, :, None] * grad_out[:, None, :])
        .astype(jnp.bfloat16)
        .reshape(-1, model_width)
    )
    padded_grads = jnp.concatenate([grad_entries, jnp.zeros((1, model_width), jnp.bfloat16)])
    grad_outgoing = padded_grads[slot_table].reshape(shard_count, E // shard_count, -1, model_width)
    grad_arrived = lax.all_to_all(grad_outgoing, "shard", split_axis=0, concat_axis=0, tiled=True)
    grad_middle = jnp.einsum(
        "nerd,efd->nerf", grad_arrived, expert_down, preferred_element_type=jnp.float32
    )
    grad_gate_part = grad_middle * up_part * gate_sigmoid * (1.0 + gate_part * (1.0 - gate_sigmoid))
    grad_up_part = grad_middle * gate_part * gate_sigmoid
    grad_gate_up_low = jnp.concatenate([grad_gate_part, grad_up_part], axis=-1).astype(jnp.bfloat16)
    grad_gate_up = jnp.einsum(
        "nerd,nerf->edf", arrived, grad_gate_up_low, preferred_element_type=jnp.float32
    )
    grad_down = jnp.einsum(
        "nerf,nerd->efd", middle, grad_arrived, preferred_element_type=jnp.float32
    )
    grad_dispatch = jnp.einsum(
        "nerf,edf->nerd", grad_gate_up_low, expert_gate_up, preferred_element_type=jnp.float32
    ).astype(jnp.bfloat16)
    upstream_cotangent_given = lax.all_to_all(
        grad_dispatch, "shard", split_axis=0, concat_axis=0, tiled=True
    ).reshape(-1, model_width)
    grad_expert_in = jnp.sum(
        upstream_cotangent_given[entry_slot]
        .reshape(token_count, TOPK, model_width)
        .astype(jnp.float32),
        axis=1,
    )
    grad_expert_in = grad_expert_in + jnp.einsum(
        "te,de->td", grad_logits, full_router, preferred_element_type=jnp.float32
    )
    grad_w_router = jnp.einsum(
        "td,te->de", expert_in, grad_logits, preferred_element_type=jnp.float32
    )
    grad_norm_two, grad_gain_experts = norm_back(
        residual_stream,
        scale_two,
        second_gain,
        grad_expert_in.reshape(seq_count, block_len, model_width),
    )
    grad_residual = grad_norm_two + grad_out.reshape(seq_count, block_len, model_width)
    softmax_mixing_cotangent = grad_residual.astype(jnp.bfloat16)
    grad_w_output = jnp.einsum(
        "fnh,fnm->hm",
        attention_result,
        softmax_mixing_cotangent,
        preferred_element_type=jnp.float32,
    )
    grad_attended = jnp.einsum(
        "hno,po->hnp",
        softmax_mixing_cotangent,
        entire_head_merge_map,
        preferred_element_type=jnp.float32,
    ).astype(jnp.bfloat16)
    grad_groups = grad_attended.reshape(seq_count, block_len, KVH, group_size, HD)
    weights = jnp.exp(score_block() - log_total)
    grad_weights = jnp.einsum(
        "sqkgd,slkd->skgql", grad_groups, values_all, preferred_element_type=jnp.float32
    )
    row_inner = jnp.sum(weights * grad_weights, axis=-1, keepdims=True)
    grad_scores = (weights * (grad_weights - row_inner)).astype(jnp.bfloat16)
    grad_query_rot = jnp.einsum(
        "skgql,slkd->sqkgd", grad_scores, keys_all, preferred_element_type=jnp.float32
    ) * HD ** (-0.5)
    grad_key_all = jnp.einsum(
        "skgql,sqkgd->slkd", grad_scores, query_groups, preferred_element_type=jnp.float32
    ) * HD ** (-0.5)
    grad_value_all = jnp.einsum(
        "skgql,sqkgd->slkd", weights_low, grad_groups, preferred_element_type=jnp.float32
    )
    local_lookup_cotangent, grad_value_own = tuple(
        (
            part.astype(jnp.float32)
            for part in side_by_side_2(
                (
                    grad_key_all.reshape(seq_count, SEQ_LEN, kv_width).astype(jnp.bfloat16),
                    grad_value_all.reshape(seq_count, SEQ_LEN, kv_width).astype(jnp.bfloat16),
                ),
                "ctx",
                1,
                0,
            )
        )
    )
    grad_query_norm = rotate_back(
        grad_query_rot.reshape(seq_count, block_len, H, HD), cosine, sine_table
    ).reshape(seq_count, block_len, model_width)
    grad_queries, grad_gain_query = norm_back(query_rows, scale_query, query_gain, grad_query_norm)
    grad_key_norm = rotate_back(
        local_lookup_cotangent.reshape(seq_count, block_len, KVH, HD), cosine, sine_table
    ).reshape(seq_count, block_len, kv_width)
    grad_keys, grad_gain_key = norm_back(keys_raw, scale_key, key_gain, grad_key_norm)
    query_gradient_narrow = grad_queries.astype(jnp.bfloat16)
    keyval_gradient_narrow = jnp.concatenate([grad_keys, grad_value_own], axis=-1).astype(
        jnp.bfloat16
    )
    query_weight_gradient = jnp.einsum(
        "fnh,fnm->hm", normalized_rows, query_gradient_narrow, preferred_element_type=jnp.float32
    )
    grad_w_keyval = jnp.einsum(
        "fnh,fnm->hm", normalized_rows, keyval_gradient_narrow, preferred_element_type=jnp.float32
    )
    grad_normed = jnp.einsum(
        "hno,po->hnp",
        query_gradient_narrow,
        complete_query_proj,
        preferred_element_type=jnp.float32,
    )
    grad_normed = grad_normed + jnp.einsum(
        "hno,po->hnp",
        keyval_gradient_narrow,
        complete_keyval_proj,
        preferred_element_type=jnp.float32,
    )
    grad_norm_one, grad_gain_attention = norm_back(layer_inputs, scale_one, first_gain, grad_normed)
    grad_input = (grad_norm_one + grad_residual).astype(jnp.bfloat16)
    dense_grads = (
        grad_gain_attention,
        query_weight_gradient,
        grad_w_keyval,
        grad_gain_query,
        grad_gain_key,
        grad_w_output,
        grad_gain_experts,
        grad_w_router,
    )
    shard_parts = (
        *tuple(
            (
                part.astype(jnp.float32)
                for part in side_by_side_3(
                    (
                        dense_grads[0].astype(jnp.bfloat16),
                        dense_grads[1].astype(jnp.bfloat16),
                        dense_grads[2].astype(jnp.bfloat16),
                        dense_grads[3].astype(jnp.bfloat16),
                    ),
                    "shard",
                    0,
                    1,
                )
            )
        ),
        lax.psum_scatter(
            dense_grads[4].astype(jnp.bfloat16), "shard", scatter_dimension=0, tiled=True
        ).astype(jnp.float32),
        *tuple(
            (
                part.astype(jnp.float32)
                for part in side_by_side_3(
                    (
                        dense_grads[5].astype(jnp.bfloat16),
                        dense_grads[6].astype(jnp.bfloat16),
                        dense_grads[7].astype(jnp.bfloat16),
                    ),
                    "shard",
                    0,
                    1,
                )
            )
        ),
    )
    dense_parts = (
        of_everyone(shard_parts[0].astype(jnp.bfloat16), "ctx").astype(jnp.float32),
        of_everyone(shard_parts[1].astype(jnp.bfloat16), "ctx").astype(jnp.float32),
        of_everyone(shard_parts[2].astype(jnp.bfloat16), "ctx").astype(jnp.float32),
        of_everyone(shard_parts[3].astype(jnp.bfloat16), "ctx").astype(jnp.float32),
        of_everyone(shard_parts[4].astype(jnp.bfloat16), "ctx").astype(jnp.float32),
        of_everyone(shard_parts[5].astype(jnp.bfloat16), "ctx").astype(jnp.float32),
        of_everyone(shard_parts[6].astype(jnp.bfloat16), "ctx").astype(jnp.float32),
        of_everyone(shard_parts[7].astype(jnp.bfloat16), "ctx").astype(jnp.float32),
    )
    expert_parts = tuple(
        (
            part.astype(jnp.float32)
            for part in one_scatter(
                (grad_gate_up.astype(jnp.bfloat16), grad_down.astype(jnp.bfloat16)), "ctx", (1, 2)
            )
        )
    )
    return (
        layer_out,
        grad_input,
        dense_parts[0],
        dense_parts[1],
        dense_parts[2],
        dense_parts[3],
        dense_parts[4],
        dense_parts[5],
        dense_parts[6],
        dense_parts[7],
        expert_parts[0],
        expert_parts[1],
    )


def solution(mesh):
    return jax.shard_map(
        local,
        mesh=mesh,
        in_specs=(
            P("shard", "ctx", None),
            P("shard", "ctx", None),
            P("shard"),
            P("shard"),
            P("shard", None),
            P("shard", None),
            P("shard"),
            P("shard"),
            P("shard", None),
            P("shard"),
            P("shard", None),
            P("shard", "ctx", None),
            P("shard", None, "ctx"),
            P("shard", "ctx", None),
        ),
        out_specs=(
            P("shard", "ctx", None),
            P("shard", "ctx", None),
            P("shard"),
            P("shard", None),
            P("shard", None),
            P("shard"),
            P("shard"),
            P("shard", None),
            P("shard"),
            P("shard", None),
            P("shard", "ctx", None),
            P("shard", None, "ctx"),
        ),
        check_vma=False,
    )
```

profile of v0, /device:TPU:2, one launch (start us, length us, event | category | flops | bytes accessed | tf_op | source)
XLA Modules:
  0.0 1024.0 jit_solution(5362306761221664925)
XLA Ops:
  16.9 27.8 %all-reduce.2 = bf16[512]{0:T(512)(128)(2,1)S(1)} all-reduce(bf16[512]{0:T(512)(128)(2,1)S(1)} %dynamic-update-slice), channel_id=1, replica_groups=mesh['shard'=16,'ctx'=8] {'shard'}, use_global_device_ids=true, to_apply=%add.2 | all-reduce | flops 512 | bytes 2048
  60.1 18.0 %reduce-window.6 = s32[2,32,8,128]{3,2,1,0:T(8,128)S(1)} reduce-window(s32[2,32,8,128]{3,2,1,0:T(8,128)S(1)} %fusion.58, s32[]{:T(128)} %constant.70.clone.1), window={size=1x1x1x128 pad=0_0x0_0x0_0x127_0}, to_apply=%region_9.10 | reduce-window | flops 8323072 | bytes 524292 | tf_op jit(solution)/shard_map/reduce-window
  93.5 67.9 %all-gather.7.cloned.1.call-done = bf16[4,1024,512]{2,1,0:T(8,128)(2,1)} async-done(((bf16[4,128,512]{2,1,0:T(8,128)(2,1)}), bf16[4,1024,512]{2,1,0:T(8,128)(2,1)}) %all-gather.7.cloned.1.call-update) | async-done | bytes 4194320 | tf_op jit(solution)/shard_map/all_gather | solution.py:51
  180.7 9.4 exponential_reduce_fusion
  199.2 14.0 %gather_fusion = bf16[3072,1024]{1,0:T(8,128)(2,1)} fusion(bf16[257,1024]{1,0:T(8,128)(2,1)S(1)} %concatenate.65, s32[3072]{0:T(1024)S(1)} %broadcast_clamp_fusion.1), kind=kCustom, calls=%fused_computation | custom fusion | bytes 12595200 | tf_op jit(solution)/shard_map/gather | solution.py:290
  224.9 18.6 %gather_fusion.2 = bf16[3072,1024]{1,0:T(8,128)(2,1)} fusion(bf16[2049,1024]{1,0:T(8,128)(2,1)} %concatenate.66, s32[3072]{0:T(1024)S(1)} %broadcast_clamp_fusion), kind=kCustom, calls=%fused_computation.2 | custom fusion | bytes 12595200 | tf_op jit(solution)/shard_map/gather | solution.py:324
  243.6 66.0 %all-to-all-done = bf16[16,2,96,1024]{3,2,1,0:T(8,128)(2,1)} async-done(((bf16[16,2,96,1024]{3,2,1,0:T(8,128)(2,1)}), bf16[16,2,96,1024]{3,2,1,0:T(8,128)(2,1)}, u32[]{:S(2)}, u32[]{:S(2)}) %all-to-all-start) | async-done | bytes 6291488 | tf_op jit(solution)/shard_map/all_to_all | solution.py:293
  330.9 12.6 %fusion.21 = f32[16,2,96,1024]{3,2,0,1:T(8,128)} fusion(bf16[16,2,96,1024]{3,2,1,0:T(8,128)(2,1)} %all-to-all-done, bf16[1024,2,1024]{2,0,1:T(8,128)(2,1)} %copy.254), kind=kOutput, calls=%fused_computation.44 | convolution fusion | flops 6442450944 | bytes 23068672 | tf_op jit(solution)/shard_map/nerd,edf->nerf/dot_general | solution.py:294
  343.5 45.1 %all-to-all-done.2 = bf16[16,2,96,1024]{3,2,1,0:T(8,128)(2,1)} async-done(((bf16[16,2,96,1024]{3,2,1,0:T(8,128)(2,1)}), bf16[16,2,96,1024]{3,2,1,0:T(8,128)(2,1)}, u32[]{:S(2)}, u32[]{:S(2)}) %all-to-all-start.2) | async-done | bytes 6291488 | tf_op jit(solution)/shard_map/all_to_all | solution.py:325
  388.6 12.2 %fusion.10 = (bf16[16,2,96,512]{3,2,0,1:T(8,128)(2,1)S(1)}, bf16[16,2,96,512]{3,2,0,1:T(8,128)(2,1)}, bf16[16,2,96,512]{3,2,0,1:T(8,128)(2,1)}) fusion(f32[16,2,96,1024]{3,2,0,1:T(8,128)} %fusion.21, bf16[2,512,1024,1]{2,1,3,0:T(8,128)(2,1)} %bitcast.268, bf16[16,2,96,1024]{3,2,1,0:T(8,128)(2,1)} %all-to-all-done.2), kind=kOutput, calls=%fused_computation.29 | convolution fusion | flops 3246391296 | bytes 30408704 | tf_op jit(solution)/shard_map/nerd,efd->nerf/dot_general | solution.py:326
  400.8 10.7 %convert_bitcast_fusion = bf16[16,2,96,1024]{3,2,0,1:T(8,128)(2,1)S(1)} fusion(bf16[1024,2,1024]{2,0,1:T(8,128)(2,1)} %copy.254, bf16[16,2,96,512]{3,2,0,1:T(8,128)(2,1)} %get-tuple-element.25, bf16[16,2,96,512]{3,2,0,1:T(8,128)(2,1)S(1)} %get-tuple-element.24), kind=kOutput, calls=%fused_computation.36 | convolution fusion | flops 6458179584 | bytes 16777216 | tf_op jit(solution)/shard_map/nerf,edf->nerd/dot_general | solution.py:338
  430.8 62.3 %all-to-all-done.3 = bf16[16,2,96,1024]{3,2,1,0:T(8,128)(2,1)} async-done(((bf16[16,2,96,1024]{3,2,1,0:T(8,128)(2,1)}), bf16[16,2,96,1024]{3,2,1,0:T(8,128)(2,1)}, u32[]{:S(2)}, u32[]{:S(2)}) %all-to-all-start.3) | async-done | bytes 6291488 | tf_op jit(solution)/shard_map/all_to_all | solution.py:341
  498.9 14.6 %gather_fusion.3 = bf16[2048,1024]{1,0:T(8,128)(2,1)} fusion(bf16[3072,1024]{1,0:T(8,128)(2,1)} %bitcast.58, s32[2048]{0:T(1024)S(1)} %broadcast_clamp_fusion.2), kind=kCustom, calls=%fused_computation.3 | custom fusion | bytes 8396800 | tf_op jit(solution)/shard_map/gather | solution.py:345
  519.9 50.7 %all-to-all-done.1 = bf16[16,2,96,1024]{3,2,1,0:T(8,128)(2,1)} async-done(((bf16[16,2,96,1024]{3,2,1,0:T(8,128)(2,1)}), bf16[16,2,96,1024]{3,2,1,0:T(8,128)(2,1)}, u32[]{:S(2)}, u32[]{:S(2)}) %all-to-all-start.1) | async-done | bytes 6291488 | tf_op jit(solution)/shard_map/all_to_all | solution.py:304
  570.6 14.6 %gather_fusion.1 = bf16[2048,1024]{1,0:T(8,128)(2,1)} fusion(bf16[3072,1024]{1,0:T(8,128)(2,1)} %bitcast.41, s32[2048]{0:T(1024)S(1)} %broadcast_clamp_fusion.2), kind=kCustom, calls=%fused_computation.1 | custom fusion | bytes 8396800 | tf_op jit(solution)/shard_map/gather | solution.py:307
  596.3 11.1 %bitcast_convert_fusion.5 = bf16[2,8,64,1024]{3,2,1,0:T(8,128)(2,1)} fusion(bf16[2,128,8,2,64]{1,4,3,2,0:T(8,128)(2,1)S(1)} %bitcast.276, f32[2,8,1024,128,2]{3,2,4,1,0:T(8,128)} %get-tuple-element.54, f32[2,8,2,128]{3,2,1,0:T(2,128)S(1)} %bitcast.282, pred[2,128,1024]{1,2,0:T(8,128)(4,1)S(1)} %broadcast_or_fusion), kind=kOutput, calls=%fused_computation.50 | convolution fusion | flops 554696704 | bytes 19677184 | tf_op jit(solution)/shard_map/skgql,sqkgd->slkd/dot_general | solution.py:389
  607.4 11.4 %fusion = (f32[2,8,2,128]{3,2,1,0:T(2,128)S(1)}, f32[2,8,1024,128,2]{3,2,4,1,0:T(8,128)}) fusion(f32[2,8,1024,128,2]{3,2,4,1,0:T(8,128)} %get-tuple-element.54, f32[2,8,2,128]{3,2,1,0:T(2,128)S(1)} %bitcast.283, pred[2,128,1024]{1,2,0:T(8,128)(4,1)S(1)} %broadcast_or_fusion, bf16[2,1024,8,64,1]{1,3,4,2,0:T(8,128)(2,1)S(1)} %bitcast.255, ...), kind=kOutput, calls=%fused_computation.7 | convolution fusion | flops 557838336 | bytes 36470784 | tf_op jit(solution)/shard_map/sqkgd,slkd->skgql/dot_general | solution.py:378
  622.8 12.3 %fusion.2 = bf16[2,8,2,128,1024]{3,4,2,1,0:T(8,128)(2,1)S(1)} fusion(f32[2,8,1024,128,2]{3,2,4,1,0:T(8,128)} %get-tuple-element.58, f32[2,8,1024,128,2]{3,2,4,1,0:T(8,128)} %get-tuple-element.54, f32[2,8,2,128]{3,2,1,0:T(2,128)S(1)} %get-tuple-element.57, f32[2,8,2,128]{3,2,1,0:T(2,128)S(1)} %bitcast.284, pred[2,128,1024]{1,2,0:T(8,128)(4,1)S(1)} %broadcast_or_fusion), kind=kLoop, calls=%fused_computation.9 | loop fusion | flops 25165824 | bytes 42237952 | tf_op jit(solution)/shard_map/convert_element_type | solution.py:382
  650.9 12.0 %bitcast_convert_fusion = bf16[2,1024,1024]{2,1,0:T(8,128)(2,1)} fusion(bf16[16,2,96,1024]{3,2,1,0:T(8,128)(2,1)} %all-to-all-done, bf16[16,2,96,512]{3,2,0,1:T(8,128)(2,1)} %get-tuple-element.25, bf16[16,2,96,512]{3,2,0,1:T(8,128)(2,1)} %copy-done.47), kind=kOutput, calls=%fused_computation.20 | convolution fusion | flops 6457131008 | bytes 16777216 | tf_op jit(solution)/shard_map/nerd,nerf->edf/dot_general | solution.py:332
  697.8 37.0 %reduce-scatter.9.cloned.1.call-done = bf16[4,128,512]{2,1,0:T(8,128)(2,1)} async-done(((bf16[4,1024,512]{2,1,0:T(8,128)(2,1)}), bf16[4,128,512]{2,1,0:T(8,128)(2,1)}) %reduce-scatter.9.cloned.1.call-update) | async-done | bytes 524304 | tf_op jit(solution)/shard_map/reduce_scatter | solution.py:57
  744.4 22.3 %concatenate.72 = bf16[1024,2050]{0,1:T(8,128)(2,1)} concatenate(bf16[1024,1]{0,1:T(2,128)(2,1)S(1)} %convert_element_type.313, bf16[1024,1024]{0,1:T(8,128)(2,1)} %bitcast_convert_fusion.4, bf16[1024,1024]{0,1:T(8,128)(2,1)S(1)} %bitcast_convert_fusion.3, bf16[1024,1]{0,1:T(2,128)(2,1)S(1)} %convert_element_type.317), dimensions={1} | concatenate | bytes 8396800 | tf_op jit(solution)/shard_map/concatenate | solution.py:66
  773.4 15.1 %pad_maximum_fusion.1 = bf16[8,393216]{1,0:T(8,128)(2,1)} fusion(bf16[8,131072]{1,0:T(8,128)(2,1)S(1)} %bitcast.252, bf16[8,262144]{1,0:T(8,128)(2,1)} %bitcast.245), kind=kLoop, calls=%fused_computation.24 | loop fusion | flops 12582912 | bytes 12582912 | tf_op jit(solution)/shard_map/concatenate | solution.py:95
  829.2 45.8 %all-reduce.3 = bf16[512]{0:T(512)(128)(2,1)S(1)} all-reduce(bf16[512]{0:T(512)(128)(2,1)S(1)} %get-tuple-element.18), channel_id=4, replica_groups=mesh['shard'=16,'ctx'=8] {'shard'}, use_global_device_ids=true, to_apply=%region_32.33.clone | all-reduce | flops 512 | bytes 2048
  920.0 71.8 %reduce-scatter.11.cloned.1.call-done = bf16[3072,128]{1,0:T(8,128)(2,1)} async-done(((bf16[24576,128]{1,0:T(8,128)(2,1)}), bf16[3072,128]{1,0:T(8,128)(2,1)}) %reduce-scatter.11.cloned.1.call-update) | async-done | bytes 786448 | tf_op jit(solution)/shard_map/reduce_scatter | solution.py:98
  (316 shorter events, 323.5 us)
Async XLA Ops:
  7.2 43.9 %all-gather.5.cloned.1.call-start = ((), (), s32[]{:S(2)}) async-start(), calls=%async_computation.16 | async-start | bytes 4734976 | tf_op jit(solution)/shard_map/all_gather | solution.py:27
  10.7 77.2 %all-gather.9.cloned.1.call-start = ((), (), s32[]{:S(2)}) async-start(), calls=%async_computation.18 | async-start | bytes 2506752 | tf_op jit(solution)/shard_map/all_gather | solution.py:27
  14.0 147.4 %all-gather.7.cloned.1.call-start = ((), (), s32[]{:S(2)}) async-start(), calls=%async_computation.17 | async-start | bytes 4718592 | tf_op jit(solution)/shard_map/all_gather | solution.py:51
  57.8 259.1 %all-gather.11.cloned.1.call-start = ((), (), s32[]{:S(2)}) async-start(), calls=%async_computation.19 | async-start | bytes 7077888 | tf_op jit(solution)/shard_map/all_gather | solution.py:38
  93.5 80.0 %copy-start.20 = (bf16[2,128,16,32]{1,3,2,0:T(8,128)(2,1)}, bf16[2,128,16,32]{1,3,2,0:T(8,128)(2,1)S(1)}, u32[]{:S(2)}) copy-start(bf16[2,128,16,32]{1,3,2,0:T(8,128)(2,1)S(1)} %get-tuple-element.31) | copy-start | bytes 786436
  93.5 80.0 %copy-start.22 = (bf16[2,128,16,32]{1,3,2,0:T(8,128)(2,1)}, bf16[2,128,16,32]{1,3,2,0:T(8,128)(2,1)S(1)}, u32[]{:S(2)}) copy-start(bf16[2,128,16,32]{1,3,2,0:T(8,128)(2,1)S(1)} %get-tuple-element.32) | copy-start | bytes 786436
  213.2 96.4 %all-to-all-start = ((bf16[16,2,96,1024]{3,2,1,0:T(8,128)(2,1)}), bf16[16,2,96,1024]{3,2,1,0:T(8,128)(2,1)}, u32[]{:S(2)}, u32[]{:S(2)}) async-start(bf16[16,2,96,1024]{3,2,1,0:T(8,128)(2,1)} %bitcast.243), calls=%async_computation | async-start | bytes 12582912 | tf_op jit(solution)/shard_map/all_to_all | solution.py:293
  309.6 79.0 %all-to-all-start.2 = ((bf16[16,2,96,1024]{3,2,1,0:T(8,128)(2,1)}), bf16[16,2,96,1024]{3,2,1,0:T(8,128)(2,1)}, u32[]{:S(2)}, u32[]{:S(2)}) async-start(bf16[16,2,96,1024]{3,2,1,0:T(8,128)(2,1)} %bitcast.244), calls=%async_computation.2 | async-start | bytes 12582912 | tf_op jit(solution)/shard_map/all_to_all | solution.py:325
  415.4 77.7 %all-to-all-start.3 = ((bf16[16,2,96,1024]{3,2,1,0:T(8,128)(2,1)}), bf16[16,2,96,1024]{3,2,1,0:T(8,128)(2,1)}, u32[]{:S(2)}, u32[]{:S(2)}) async-start(bf16[16,2,96,1024]{3,2,1,0:T(8,128)(2,1)} %copy.264), calls=%async_computation.3 | async-start | bytes 12582912 | tf_op jit(solution)/shard_map/all_to_all | solution.py:341
  493.1 77.5 %all-to-all-start.1 = ((bf16[16,2,96,1024]{3,2,1,0:T(8,128)(2,1)}), bf16[16,2,96,1024]{3,2,1,0:T(8,128)(2,1)}, u32[]{:S(2)}, u32[]{:S(2)}) async-start(bf16[16,2,96,1024]{3,2,1,0:T(8,128)(2,1)} %copy.261), calls=%async_computation.1 | async-start | bytes 12582912 | tf_op jit(solution)/shard_map/all_to_all | solution.py:304
  498.8 236.0 %reduce-scatter.9.cloned.1.call-start = ((), (), s32[]{:S(2)}) async-start(), calls=%async_computation.20 | async-start | bytes 4718592 | tf_op jit(solution)/shard_map/reduce_scatter | solution.py:57
  595.3 67.9 %copy-start.5 = (f32[2,128,1024]{2,1,0:T(8,128)}, f32[2,128,1024]{2,1,0:T(8,128)S(1)}, u32[]{:S(2)}) copy-start(f32[2,128,1024]{2,1,0:T(8,128)S(1)} %get-tuple-element.33) | copy-start | bytes 3145732
  650.9 147.2 %reduce-scatter.15.cloned.1.call-start = ((), (), s32[]{:S(2)}) async-start(), calls=%async_computation.23 | async-start | bytes 2506752
  675.7 206.4 %reduce-scatter.13.cloned.1.call-start = ((), (), s32[]{:S(2)}) async-start(), calls=%async_computation.22 | async-start | bytes 4734976
  773.3 218.5 %reduce-scatter.11.cloned.1.call-start = ((), (), s32[]{:S(2)}) async-start(), calls=%async_computation.21 | async-start | bytes 7077888 | tf_op jit(solution)/shard_map/reduce_scatter | solution.py:98
  799.5 13.4 %all-to-all-start.10 = ((bf16[8,1,64]{2,1,0:T(2,128)(2,1)}), bf16[8,1,64]{2,1,0:T(2,128)(2,1)S(1)}, u32[]{:S(2)}, u32[]{:S(2)}) async-start(bf16[8,1,64]{2,1,0:T(2,128)(2,1)} %broadcast_in_dim.77), calls=%async_computation.11 | async-start | bytes 8192 | tf_op jit(solution)/shard_map/all_to_all | solution.py:78
  812.9 11.0 %all-to-all-start.11 = ((bf16[8,2,1024]{2,1,0:T(2,128)(2,1)}), bf16[8,2,1024]{2,1,0:T(2,128)(2,1)S(1)}, u32[]{:S(2)}, u32[]{:S(2)}) async-start(bf16[8,2,1024]{2,1,0:T(2,128)(2,1)} %reshape.802), calls=%async_computation.12 | async-start | bytes 65536 | tf_op jit(solution)/shard_map/all_to_all | solution.py:78
  825.0 50.1 %all-to-all-start.9 = ((bf16[8,64,1024]{2,1,0:T(8,128)(2,1)}), bf16[8,64,1024]{2,1,0:T(8,128)(2,1)S(1)}, u32[]{:S(2)}, u32[]{:S(2)}) async-start(bf16[8,64,1024]{2,1,0:T(8,128)(2,1)} %broadcast_in_dim.75), calls=%async_computation.10 | async-start | bytes 2097152 | tf_op jit(solution)/shard_map/all_to_all | solution.py:78
  875.7 13.9 %all-to-all-start.8 = ((bf16[8,1,32]{2,1,0:T(2,128)(2,1)}), bf16[8,1,32]{2,1,0:T(2,128)(2,1)S(1)}, u32[]{:S(2)}, u32[]{:S(2)}) async-start(bf16[8,1,32]{2,1,0:T(2,128)(2,1)} %broadcast_in_dim.74), calls=%async_computation.9 | async-start | bytes 8192 | tf_op jit(solution)/shard_map/all_to_all | solution.py:78
  890.2 10.8 %all-to-all-start.7 = ((bf16[8,1,64]{2,1,0:T(2,128)(2,1)}), bf16[8,1,64]{2,1,0:T(2,128)(2,1)S(1)}, u32[]{:S(2)}, u32[]{:S(2)}) async-start(bf16[8,1,64]{2,1,0:T(2,128)(2,1)} %broadcast_in_dim.73), calls=%async_computation.8 | async-start | bytes 8192 | tf_op jit(solution)/shard_map/all_to_all | solution.py:78
  901.6 10.8 %all-to-all-start.4 = ((bf16[8,1,64]{2,1,0:T(2,128)(2,1)}), bf16[8,1,64]{2,1,0:T(2,128)(2,1)S(1)}, u32[]{:S(2)}, u32[]{:S(2)}) async-start(bf16[8,1,64]{2,1,0:T(2,128)(2,1)} %broadcast_in_dim.69), calls=%async_computation.5 | async-start | bytes 8192 | tf_op jit(solution)/shard_map/all_to_all | solution.py:78
  912.5 88.7 %copy-start.6 = (f32[2,128,1024]{2,1,0:T(8,128)S(1)}, f32[2,128,1024]{2,1,0:T(8,128)}, u32[]{:S(2)}) copy-start(f32[2,128,1024]{2,1,0:T(8,128)} %copy-done.5) | copy-start | bytes 3145732
  913.6 82.3 %all-to-all-start.6 = ((bf16[8,64,1024]{2,1,0:T(8,128)(2,1)}), bf16[8,64,1024]{2,1,0:T(8,128)(2,1)}, u32[]{:S(2)}, u32[]{:S(2)}) async-start(bf16[8,64,1024]{2,1,0:T(8,128)(2,1)} %broadcast_in_dim.71), calls=%async_computation.7 | async-start | bytes 2097152 | tf_op jit(solution)/shard_map/all_to_all | solution.py:78
  997.0 19.0 %all-to-all-start.5 = ((bf16[8,64,1024]{2,1,0:T(8,128)(2,1)}), bf16[8,64,1024]{2,1,0:T(8,128)(2,1)S(1)}, u32[]{:S(2)}, u32[]{:S(2)}) async-start(bf16[8,64,1024]{2,1,0:T(8,128)(2,1)} %broadcast_in_dim.70), calls=%async_computation.6 | async-start | bytes 2097152 | tf_op jit(solution)/shard_map/all_to_all | solution.py:78
  (46 other events, 656.9 us)
Sparse Core Ops, SparseCore 0:
  10.8 40.2 all-gather.4
  53.3 34.4 all-gather.8
  90.7 70.6 all-gather.6
  164.0 112.9 all-gather.10
  651.0 83.8 reduce-scatter.8
  737.2 60.8 reduce-scatter.14
  800.6 76.9 reduce-scatter.12
  881.4 110.3 reduce-scatter.10
where the time goes:
time: 1030 us; the launch traced here: 1020 us
  waiting for transfers between devices  449 us (44%)
  local copies, waits for them, and re-layouts  200 us (19%)
  matrix products  127 us (12%)
  other arithmetic  96.4 us (9%)
  blocking collectives  73.6 us (7%)
  starting transfers between devices  60.4 us (6%)
  between operations  17 us (2%)
    unnamed x2, blocking collectives  73.6 us
    reduce_scatter x1, waiting for transfers between devices, one_scatter(): lax.psum_scatter(lines, axis, tiled=True).reshape(-1)  71.8 us
    all_gather x1, waiting for transfers between devices, side_by_side(): result = lax.all_gather(both, axis, axis=dim, tiled=True)  67.9 us
    all_to_all x1, waiting for transfers between devices, local(): lax.all_to_all(outgoing, 'shard', split_axis=0, concat_axis=0, tiled=True)  66 us
    all_to_all x1, waiting for transfers between devices, local(): lax.all_to_all(grad_dispatch, 'shard', split_axis=0, concat_axis=0, tiled...  62.3 us
    all_to_all x1, waiting for transfers between devices, local(): lax.all_to_all(expert_out, 'shard', split_axis=0, concat_axis=0, tiled=True)  50.7 us
    all_to_all x1, waiting for transfers between devices, local(): lax.all_to_all(grad_outgoing, 'shard', split_axis=0, concat_axis=0, tiled...  45.1 us
    all_to_all x8, waiting for transfers between devices, copy_for_each(): lax.all_to_all(jnp.broadcast_to(array[None], (count, *array.shape)), axis...  42 us
  transfers between devices with their start and end apart: 20, of which 16 were waited for; matrix products, arithmetic and copies ran while one was open for 30% of the time, Pallas kernels for 0%

commit v1 on v0

v1 whole, which is shorter than its diff:
```python
import functools

import jax
import jax.numpy as jnp
from jax import lax
from jax.experimental import pallas as pl
from jax.experimental.pallas import tpu as pltpu
from jax.sharding import PartitionSpec as P

D = 1024
KVH = 8
HD = 64
FF = 512
E = 32
SEQ_LEN = 1024
BLK = 128
SEQS = 2
ROWS = SEQS * BLK
CAP = 48
SLOTS = 4 * CAP
N_SHARD = 16
N_CTX = 8
PAIRS = 8
LANE = 128
QB = 256
EPSILON = 1e-06
ROPE_BASE = 10000.0
MASKED = -1e30
F32 = jnp.float32
BF16 = jnp.bfloat16

LANES = [[c + 2 * k for k in range(PAIRS)] for c in range(2)]
CHIPS = [[(c + 2 * k) * N_CTX + j for k in range(PAIRS) for j in range(N_CTX)] for c in range(2)]
OTHER_CORE = [(i, i ^ 1) for i in range(N_SHARD)]
X_HI = [(i, i ^ 4) for i in range(N_CTX)]
FIRST = 2 * D + 2 * LANE
LAST = 2 * D + LANE


def y_shift(step):
    return [(i, i // 4 * 4 + (i + step) % 4) for i in range(N_CTX)]


def dot(a, b):
    return jnp.dot(a, b, preferred_element_type=F32)


def dot_nt(a, b):
    return lax.dot_general(a, b, (((1,), (1,)), ((), ())), preferred_element_type=F32)


def dot_tn(a, b):
    return lax.dot_general(a, b, (((0,), (0,)), ((), ())), preferred_element_type=F32)


def lane_of(shape):
    return lax.broadcasted_iota(jnp.int32, shape, len(shape) - 1)


def inverse_scale(z):
    return lax.rsqrt(jnp.mean(z * z, axis=-1, keepdims=True) + EPSILON)


def swap_halves(x):
    first = lane_of(x.shape) % HD < HD // 2
    return jnp.where(first, pltpu.roll(x, LANE - HD // 2, 1), pltpu.roll(x, HD // 2, 1))


def side(h):
    return slice(h * LANE, (h + 1) * LANE)


def kernel_call(body, out, flops=0, nbytes=0, mb=48, **kwargs):
    return pl.pallas_call(
        body,
        out_shape=out,
        compiler_params=pltpu.CompilerParams(vmem_limit_bytes=mb * 2**20),
        cost_estimate=pl.CostEstimate(flops=flops, bytes_accessed=nbytes, transcendentals=0),
        **kwargs,
    )


def struct(shape, dtype):
    return jax.ShapeDtypeStruct(shape, dtype)


def key_lanes(shape):
    return lane_of(shape) % LANE < HD


def kv_scale(kv_raw):
    keys = key_lanes(kv_raw.shape)
    total = jnp.sum(jnp.where(keys, kv_raw * kv_raw, 0.0), axis=-1, keepdims=True)
    return lax.rsqrt(total / (D // 2) + EPSILON), keys


def turned_gains(block):
    rows = block.astype(F32).T[0:8]
    place = lane_of(rows.shape) % LANE
    keys = jnp.where(place < HD // 2, rows, pltpu.roll(rows, D - HD // 2, 1))
    keys = jnp.where(place < HD, keys, 1.0)
    which = lax.broadcasted_iota(jnp.int32, rows.shape, 0)
    return jnp.where(which == 2, keys, rows)


def front_body(x_ref, w_ref, rope_ref, packed_ref, normed_ref, q_ref, kv_ref, gains_ref):
    x = x_ref[...].astype(F32)
    gains = turned_gains(w_ref[:, LAST:FIRST])
    gains_ref[...] = gains
    normed = (x * inverse_scale(x) * gains[0:1]).astype(BF16)
    normed_ref[...] = normed
    q = dot(normed, w_ref[:, 0:D])
    kv = dot(normed, w_ref[:, D : 2 * D])
    q_ref[...] = q
    kv_ref[...] = kv
    r_k, keys = kv_scale(kv)
    qn = q * inverse_scale(q) * gains[1:2]
    kn = kv * jnp.where(keys, r_k * gains[2:3], 1.0)
    c, s, ck, sk = rope_ref[0], rope_ref[1], rope_ref[2], rope_ref[3]
    for h in range(KVH):
        qh, kh = qn[:, side(h)], kn[:, side(h)]
        packed_ref[h, :, 0:LANE] = (qh * c + swap_halves(qh) * s).astype(BF16)
        packed_ref[h, :, LANE : 2 * LANE] = (kh * ck + swap_halves(kh) * sk).astype(BF16)


def front(x, first, rope):
    return kernel_call(
        front_body,
        (
            struct((KVH, ROWS, 2 * LANE), BF16),
            struct((ROWS, D), BF16),
            struct((ROWS, D), F32),
            struct((ROWS, D), F32),
            struct((8, D), F32),
        ),
        flops=2 * ROWS * D * 2 * D,
        nbytes=9 * 2**20,
    )(x, first, rope)


def key_extent(qb):
    return max((qb + 1) * QB, SEQ_LEN // 2)


def both_halves(kv):
    kv = kv.astype(F32)
    turned = pltpu.roll(kv, HD, 1)
    low = lane_of(kv.shape) < HD
    return jnp.where(low, kv, turned).astype(BF16), jnp.where(low, turned, kv).astype(BF16)


def attend_body(prefix_ref, in_ref, out_ref):
    length = prefix_ref[pl.program_id(0)]
    rows = in_ref[...].reshape(SEQ_LEN, 2 * LANE)
    q = rows[:, :LANE] * jnp.asarray(HD**-0.5, BF16)
    k2, v2 = both_halves(rows[:, LANE:])
    group = lane_of((SEQ_LEN, LANE)) // HD
    zero = jnp.zeros((), BF16)
    values = [jnp.where(group == g, v2, zero) for g in range(2)]
    for qb in range(SEQ_LEN // QB):
        lo, hi = qb * QB, key_extent(qb)
        i = lo + lax.broadcasted_iota(jnp.int32, (QB, hi - lo), 0)
        j = lo + lane_of((QB, hi - lo))
        seen = (j <= i) | (j < length)
        total = jnp.zeros((QB, LANE), F32)
        for g in range(2):
            qg = jnp.where(group[lo : lo + QB] == g, q[lo : lo + QB], zero)
            near = jnp.where(seen, dot_nt(qg, k2[lo:hi]), MASKED)
            peak = jnp.max(near, axis=1, keepdims=True)
            if lo:
                far = dot_nt(qg, k2[:lo])
                peak = jnp.maximum(peak, jnp.max(far, axis=1, keepdims=True))
            near = jnp.exp(near - peak)
            norm = jnp.sum(near, axis=1, keepdims=True)
            out = dot(near.astype(BF16), values[g][lo:hi])
            if lo:
                far = jnp.exp(far - peak)
                norm = norm + jnp.sum(far, axis=1, keepdims=True)
                out = out + dot(far.astype(BF16), values[g][:lo])
            total = total + out / norm
        out_ref[2 * qb : 2 * qb + 2] = total.astype(BF16).reshape(2, BLK, LANE)


def attend(prefix, rows):
    return kernel_call(
        attend_body,
        struct((N_CTX, ROWS, LANE), BF16),
        flops=2 * 2 * 2 * 1024 * 1024 * 128,
        nbytes=2 * 2**20,
        grid=(SEQS,),
        in_specs=[
            pl.BlockSpec(memory_space=pltpu.SMEM),
            pl.BlockSpec((N_CTX, BLK, 2 * LANE), lambda s: (0, s, 0)),
        ],
        out_specs=pl.BlockSpec((N_CTX, BLK, LANE), lambda s: (0, s, 0)),
    )(prefix, rows)


def attend_back_body(prefix_ref, in_ref, grad_ref, out_ref, dk_ref, dv_ref):
    length = prefix_ref[pl.program_id(0)]
    rows = in_ref[...].reshape(SEQ_LEN, 2 * LANE)
    q = rows[:, :LANE] * jnp.asarray(HD**-0.5, BF16)
    k2, v2 = both_halves(rows[:, LANE:])
    grad = grad_ref[...].reshape(SEQ_LEN, LANE)
    group = lane_of((SEQ_LEN, LANE)) // HD
    zero = jnp.zeros((), BF16)
    keys = [jnp.where(group == g, k2, zero) for g in range(2)]
    dk_ref[...] = jnp.zeros_like(dk_ref)
    dv_ref[...] = jnp.zeros_like(dv_ref)
    for qb in range(SEQ_LEN // QB):
        lo, hi = qb * QB, key_extent(qb)
        i = lo + lane_of((hi - lo, QB))
        j = lo + lax.broadcasted_iota(jnp.int32, (hi - lo, QB), 0)
        seen = (j <= i) | (j < length)
        dq = jnp.zeros((QB, LANE), F32)
        for g in range(2):
            mine = group[lo : lo + QB] == g
            qg = jnp.where(mine, q[lo : lo + QB], zero)
            gg = jnp.where(mine, grad[lo : lo + QB], zero)
            spans = [(lo, hi)] + ([(0, lo)] if lo else [])
            scores = [dot_nt(k2[a:b], qg) for a, b in spans]
            scores[0] = jnp.where(seen, scores[0], MASKED)
            peak = functools.reduce(jnp.maximum, [jnp.max(s, axis=0, keepdims=True) for s in scores])
            scores = [jnp.exp(s - peak) for s in scores]
            norm = 1.0 / sum(jnp.sum(s, axis=0, keepdims=True) for s in scores)
            scores = [s * norm for s in scores]
            grads = [dot_nt(v2[a:b], gg) for a, b in spans]
            inner = sum(jnp.sum(s * d, axis=0, keepdims=True) for s, d in zip(scores, grads))
            for (a, b), s, d in zip(spans, scores, grads):
                ds = (s * (d - inner)).astype(BF16)
                dv_ref[a:b] += dot(s.astype(BF16), gg)
                dk_ref[a:b] += dot(ds, qg)
                dq = dq + dot_tn(ds, keys[g][a:b])
        out_ref[2 * qb : 2 * qb + 2, :, 0:LANE] = (dq * HD**-0.5).astype(BF16).reshape(2, BLK, LANE)
    dk = dk_ref[...]
    dv = dv_ref[...]
    dk = dk + pltpu.roll(dk, HD, 1)
    dv = dv + pltpu.roll(dv, HD, 1)
    out = jnp.where(lane_of(dk.shape) < HD, dk, dv).astype(BF16)
    out_ref[:, :, LANE : 2 * LANE] = out.reshape(N_CTX, BLK, LANE)


def attend_back(prefix, rows, grad):
    return kernel_call(
        attend_back_body,
        struct((N_CTX, ROWS, 2 * LANE), BF16),
        flops=2 * 5 * 2 * 1024 * 1024 * 128,
        nbytes=3 * 2**20,
        grid=(SEQS,),
        in_specs=[
            pl.BlockSpec(memory_space=pltpu.SMEM),
            pl.BlockSpec((N_CTX, BLK, 2 * LANE), lambda s: (0, s, 0)),
            pl.BlockSpec((N_CTX, BLK, LANE), lambda s: (0, s, 0)),
        ],
        out_specs=pl.BlockSpec((N_CTX, BLK, 2 * LANE), lambda s: (0, s, 0)),
        scratch_shapes=[pltpu.VMEM((SEQ_LEN, LANE), F32), pltpu.VMEM((SEQ_LEN, LANE), F32)],
    )(prefix, rows, grad)


def middle_body(x_ref, att_ref, wo_ref, gains_ref, residual_ref, attended_ref, in_ref, copy_ref):
    for h in range(KVH):
        attended_ref[:, side(h)] = att_ref[h]
    wo = wo_ref[:, :, 0:D].reshape(D, D)
    copy_ref[...] = wo
    residual = x_ref[...].astype(F32) + dot(attended_ref[...], wo)
    residual_ref[...] = residual
    in_ref[...] = (residual * inverse_scale(residual) * gains_ref[3:4]).astype(BF16)


def middle(x, att, all_out, gains):
    full = lambda *shape: pl.BlockSpec(shape, lambda i: (0,) * len(shape))
    return kernel_call(
        middle_body,
        (struct((ROWS, D), F32), struct((ROWS, D), BF16), struct((ROWS, D), BF16), struct((D, D), BF16)),
        flops=2 * ROWS * D * D,
        nbytes=7 * 2**20,
        grid=(1,),
        in_specs=[
            full(ROWS, D),
            full(KVH, ROWS, LANE),
            pl.BlockSpec((N_SHARD, 64, D + LANE), lambda i: (0, ROWS // 64, 0)),
            full(8, D),
        ],
        out_specs=(full(ROWS, D),) * 3 + (full(D, D),),
    )(x, att, all_out, gains)


def softmax_over(logits, member):
    logits = jnp.where(member, logits, MASKED)
    e = jnp.exp(logits - jnp.max(logits, axis=-1, keepdims=True))
    return e / jnp.sum(e, axis=-1, keepdims=True)


def split_two(v):
    high = v.astype(BF16)
    return high, (v - high.astype(F32)).astype(BF16)


def experts_body(
    me_ref, x_ref, g_ref, slot_ref, router_ref, p0, p1, p2, p3, p4, p5, p6, p7,
    back_keep, back_give, out_ref, gg_ref, xr_ref, go_ref, mid_ref, dgu_ref,
    wo_ref, gd_ref, gr_ref, w_ref, sem,
):
    shard = me_ref[0]

    @pl.when(pl.program_id(0) == 0)
    def _():
        copies = []
        for n, piece in enumerate((p0, p1, p2, p3, p4, p5, p6, p7)):
            at = pl.multiple_of(me_ref[1 + n] * BLK, BLK)
            for e in range(2):
                copies.append(
                    pltpu.make_async_copy(piece.at[e], w_ref.at[e, pl.ds(at, BLK)], sem.at[2 * n + e])
                )
        for copy in copies:
            copy.start()
        for copy in copies:
            copy.wait()

    core = lax.rem(shard, 2)
    sources = [(k, j, lax.rem(core + j, 2)) for k in range(2) for j in range(2)]
    picks = []
    for n, (k, j, c) in enumerate(sources):
        slots = slot_ref[k, c]
        want = lax.broadcasted_iota(jnp.int32, (2 * CAP, ROWS), 0).astype(F32)
        pick = jnp.concatenate(
            [(slots[e : e + 1] == want).astype(F32) for e in range(2)], axis=0
        ).astype(BF16)
        picks.append(pick)
        x = x_ref[k, c]
        grads = g_ref[k, c, :, 0:D]
        member = g_ref[k, c, :, D : D + LANE].astype(F32) > 0
        gates = softmax_over(dot(x, router_ref[...]), member)
        high, low = split_two(gates)
        at = dot(pick, high) + dot(pick, low)
        lane = lane_of(at.shape) - shard * 8
        expert = lax.broadcasted_iota(jnp.int32, at.shape, 0) // (2 * CAP)
        gate = jnp.sum(jnp.where(lane == expert, at, 0.0), axis=-1, keepdims=True)
        rows = dot(pick, x).astype(BF16)
        grad_rows = dot(pick, grads)
        scaled = (gate * grad_rows).astype(BF16)
        grad_rows = grad_rows.astype(BF16)
        place = slice(n * 2 * CAP, (n + 1) * 2 * CAP)
        for e in range(2):
            part = slice(e * 2 * CAP, (e + 1) * 2 * CAP)
            xr_ref[e, place] = rows[part]
            go_ref[e, place] = scaled[part]
            gr_ref[e, place] = grad_rows[part]
            gd_ref[e, place] = jnp.broadcast_to(gate[part], (2 * CAP, LANE))
    dots = []
    for e in range(2):
        gate_up = dot(xr_ref[e], w_ref[e, :, 0 : 2 * FF])
        g, u = gate_up[:, :FF], gate_up[:, FF:]
        sig = 1.0 / (1.0 + jnp.exp(-g))
        act = g * sig
        mid = (act * u).astype(BF16)
        mid_ref[e] = mid
        out = dot_nt(mid, w_ref[e, :, 2 * FF :]).astype(BF16).astype(F32)
        dots.append(jnp.sum(out * gr_ref[e].astype(F32), axis=-1, keepdims=True))
        wo_ref[e] = (out * gd_ref[e, :, 0:1]).astype(BF16)
        grad_mid = dot(go_ref[e], w_ref[e, :, 2 * FF :])
        dgu_ref[e, :, 0:FF] = (grad_mid * u * sig * (1.0 + g * (1.0 - sig))).astype(BF16)
        dgu_ref[e, :, FF : 2 * FF] = (grad_mid * act).astype(BF16)
        gr_ref[e] = dot_nt(dgu_ref[e], w_ref[e, :, 0 : 2 * FF]).astype(BF16)
    for n, (k, j, c) in enumerate(sources):
        place = slice(n * 2 * CAP, (n + 1) * 2 * CAP)
        pick = picks[n]
        back = dot_tn(pick, jnp.concatenate([gr_ref[0, place], gr_ref[1, place]], axis=0))
        out = dot_tn(pick, jnp.concatenate([wo_ref[0, place], wo_ref[1, place]], axis=0))
        (back_give if j else back_keep)[k] = back.astype(BF16)
        out_ref[k, c] = out.astype(BF16)
        values = jnp.concatenate([dots[0][place], dots[1][place]], axis=0)
        lane = lane_of((SLOTS, LANE))
        expert = lax.broadcasted_iota(jnp.int32, (SLOTS, LANE), 0) // (2 * CAP)
        high, low = split_two(jnp.where(lane == expert, values, 0.0))
        gg_ref[k, c] = (dot_tn(high, pick) + dot_tn(low, pick))[0:8]


def experts(places, x, grads, slots, router, pieces):
    steps = 4
    per = 2 * 4 * CAP
    half = pl.BlockSpec((2, ROWS, D), lambda i: (i, 0, 0))
    kept = lambda width: pl.BlockSpec((2, per, width), lambda i: (0, i, 0))
    whole = lambda shape: pl.BlockSpec(shape, lambda i: (0,) * len(shape), pipeline_mode=pl.Buffered(1))
    total = steps * per
    return kernel_call(
        experts_body,
        (struct((PAIRS, ROWS, D), BF16),) * 2
        + (
            struct((PAIRS, 2, ROWS, D), BF16),
            struct((PAIRS, 2, 8, ROWS), F32),
            struct((2, total, D), BF16),
            struct((2, total, D), BF16),
            struct((2, total, FF), BF16),
            struct((2, total, 2 * FF), BF16),
        ),
        flops=30 * 10**9,
        nbytes=60 * 2**20,
        mb=60,
        grid=(steps,),
        in_specs=[
            pl.BlockSpec(memory_space=pltpu.SMEM),
            pl.BlockSpec((2, 2, ROWS, D), lambda i: (i, 0, 0, 0)),
            pl.BlockSpec((2, 2, ROWS, D + LANE), lambda i: (i, 0, 0, 0)),
            pl.BlockSpec((2, 2, 2, ROWS), lambda i: (i, 0, 0, 0)),
            whole((D, LANE)),
        ]
        + [pl.BlockSpec(memory_space=pl.ANY)] * 8,
        out_specs=(half,) * 2
        + (
            pl.BlockSpec((2, 2, ROWS, D), lambda i: (i, 0, 0, 0)),
            pl.BlockSpec((2, 2, 8, ROWS), lambda i: (i, 0, 0, 0)),
            kept(D), kept(D), kept(FF), kept(2 * FF),
        ),
        scratch_shapes=[
            pltpu.VMEM((2, per, D), BF16),
            pltpu.VMEM((2, per, LANE), F32),
            pltpu.VMEM((2, per, D), BF16),
            pltpu.VMEM((2, D, 3 * FF), BF16),
            pltpu.SemaphoreType.DMA((16,)),
        ],
    )(places, x, grads, slots, router, *pieces)


def expert_grads_body(me_ref, xa_ref, xb_ref, ga_ref, gb_ref, mid_ref, dgu_ref, *out_refs):
    values = []
    for e in range(2):
        rows = jnp.concatenate([xa_ref[e], xb_ref[e]], axis=1)
        values.append(dot_tn(rows, dgu_ref[e]).astype(BF16))
        rows = jnp.concatenate([ga_ref[e], gb_ref[e]], axis=1)
        values.append(dot_tn(rows, mid_ref[e]).astype(BF16))
    for step, out_ref in enumerate(out_refs):

        @pl.when(pl.program_id(0) == step)
        def _():
            for e in range(2):
                for half in range(2):
                    part = slice(half * BLK, (half + 1) * BLK)
                    out_ref[half, e, :, 0 : 2 * FF] = values[2 * e][part]
                    out_ref[half, e, :, 2 * FF :] = values[2 * e + 1][part]


def expert_grads(places, rows_in, rows_grad, mid, dgu):
    total = rows_in.shape[1]
    column = lambda half: pl.BlockSpec((2, total, BLK), lambda t, me: (0, 0, me[1 + 2 * t + half]))
    whole = lambda width: pl.BlockSpec((2, total, width), lambda t, me: (0, 0, 0))
    piece = (2, 2, BLK, 3 * FF)
    return kernel_call(
        expert_grads_body,
        (struct(piece, BF16),) * 4,
        flops=2 * 2 * total * D * 3 * FF,
        nbytes=30 * 2**20,
        grid_spec=pltpu.PrefetchScalarGridSpec(
            num_scalar_prefetch=1,
            grid=(4,),
            in_specs=[column(0), column(1), column(0), column(1), whole(FF), whole(2 * FF)],
            out_specs=(pl.BlockSpec(piece, lambda t, me: (0, 0, 0, 0)),) * 4,
        ),
    )(places, rows_in, rows_in, rows_grad, rows_grad, mid, dgu)


def norm_back(z, r, gain, grad):
    weighted = grad * gain
    inner = jnp.mean(weighted * z, axis=-1, keepdims=True)
    return r * weighted - z * (r * r * r) * inner, jnp.sum(grad * z * r, axis=0, keepdims=True)


def turn_body(
    parts_ref, gg_ref, in_ref, residual_ref, cot_ref, routes_ref, router_ref, gains_ref, wo_ref,
    gatt_ref, gres_ref, gattn_ref, glog_ref, ggain_ref,
):
    member = routes_ref[...].astype(F32) > 0
    gates = softmax_over(dot(in_ref[...], router_ref[...]), member)
    gg = gg_ref[...].reshape(LANE, ROWS).T
    chosen = gates * (gg - jnp.sum(gates * gg, axis=-1, keepdims=True))
    glog = chosen.astype(BF16)
    glog_ref[...] = glog
    grad = dot_nt(glog, router_ref[...])
    for n in range(PAIRS):
        grad = grad + parts_ref[n].astype(F32)
    residual = residual_ref[...]
    gz, ggain = norm_back(residual, inverse_scale(residual), gains_ref[3:4], grad)
    ggain_ref[...] = ggain
    gres = cot_ref[...].astype(F32) + gz
    gres_ref[...] = gres
    gattn = gres.astype(BF16)
    gattn_ref[...] = gattn
    gatt = dot_nt(gattn, wo_ref[...]).astype(BF16)
    for h in range(KVH):
        gatt_ref[h] = gatt[:, side(h)]


def turn(parts, gg, expert_in, residual, cot, member, router, gains, wo):
    return kernel_call(
        turn_body,
        (
            struct((KVH, ROWS, LANE), BF16),
            struct((ROWS, D), F32),
            struct((ROWS, D), BF16),
            struct((ROWS, LANE), BF16),
            struct((1, D), F32),
        ),
        flops=2 * ROWS * D * D,
        nbytes=10 * 2**20,
    )(parts, gg, expert_in, residual, cot, member, router, gains, wo)


def finish_body(
    me_ref, rows_ref, q_ref, kv_ref, x_ref, normed_ref, gres_ref, w_ref, gains_ref, rope_ref, side_ref, gaine_ref,
    grad_in_ref, keep_ref, give_ref, gq_ref, gk_ref, gw_ref,
):
    core = lax.rem(me_ref[0], 2)
    gains = gains_ref[...]
    c, s, ck, sk = rope_ref[0], rope_ref[1], rope_ref[2], rope_ref[3]
    for h in range(KVH):
        gh = rows_ref[h, :, 0:LANE].astype(F32)
        kh = rows_ref[h, :, LANE : 2 * LANE].astype(F32)
        gq_ref[:, side(h)] = gh * c - swap_halves(gh) * s
        gk_ref[:, side(h)] = kh * ck - swap_halves(kh) * sk
    q = q_ref[...]
    gq, gain_q = norm_back(q, inverse_scale(q), gains[1:2], gq_ref[...])
    gq = gq.astype(BF16)
    kv, gkv = kv_ref[...], gk_ref[...]
    r, keys = kv_scale(kv)
    weighted = jnp.where(keys, gkv * gains[2:3], 0.0)
    inner = jnp.sum(weighted * kv, axis=-1, keepdims=True) / (D // 2)
    gk = jnp.where(keys, r * weighted - kv * (r * r * r) * inner, gkv).astype(BF16)
    gain_k = jnp.sum(jnp.where(keys, gkv * kv * r, 0.0), axis=0, keepdims=True)
    normed = normed_ref[...]
    gw_ref[:, :, 0:D] = dot_tn(normed, gq).astype(BF16).reshape(N_SHARD, 64, D)
    gw_ref[:, :, D : 2 * D] = dot_tn(normed, gk).astype(BF16).reshape(N_SHARD, 64, D)
    grad = dot_nt(gq, w_ref[:, 0:D]) + dot_nt(gk, w_ref[:, D : 2 * D])
    x = x_ref[...].astype(F32)
    gx, gain_a = norm_back(x, inverse_scale(x), gains[0:1], grad)
    grad_in_ref[...] = (gres_ref[...] + gx).astype(BF16)
    zero = jnp.zeros((2, D), F32)
    rows = jnp.concatenate([zero, gain_a, gain_q, gain_k, gaine_ref[...], zero], axis=0)
    which = lax.broadcasted_iota(jnp.int32, rows.shape, 0)
    place = lane_of(rows.shape) % LANE
    rows = jnp.where((which == 4) & (place >= HD), pltpu.roll(rows, HD // 2, 1), rows)
    rows = jnp.concatenate([rows, jnp.zeros((LANE - 8, D), F32)], axis=0)
    beside = (side_ref[...] + rows.T).astype(BF16)
    gw_ref[:, :, 2 * D : LAST] = beside.reshape(N_SHARD, 64, LANE)
    for k in range(PAIRS):
        keep_ref[k] = gw_ref[2 * k + core]
        give_ref[k] = gw_ref[2 * k + 1 - core]


def finish(places, rows, q, kv, x, normed, gres, first, gains, rope, beside, gain_e):
    vmem = pl.BlockSpec(memory_space=pltpu.VMEM)
    return kernel_call(
        finish_body,
        (struct((ROWS, D), BF16),) + (struct((PAIRS, 64, LAST), BF16),) * 2,
        flops=4 * 2 * ROWS * D * D,
        nbytes=15 * 2**20,
        in_specs=[pl.BlockSpec(memory_space=pltpu.SMEM)] + [vmem] * 11,
        scratch_shapes=[
            pltpu.VMEM((ROWS, D), F32),
            pltpu.VMEM((ROWS, D), F32),
            pltpu.VMEM((N_SHARD, 64, LAST), BF16),
        ],
    )(places, rows, q, kv, x, normed, gres, first, gains, rope, beside, gain_e)


def project_back_body(
    me_ref, att_ref, gattn_ref, in_ref, glog_ref, keep_ref, give_ref, beside_ref, gw_ref
):
    core = lax.rem(me_ref[0], 2)
    gw_ref[...] = dot_tn(att_ref[...], gattn_ref[...]).astype(BF16).reshape(N_SHARD, 64, D)
    for k in range(PAIRS):
        keep_ref[k] = gw_ref[2 * k + core]
        give_ref[k] = gw_ref[2 * k + 1 - core]
    beside_ref[...] = dot_tn(in_ref[...], glog_ref[...])


def project_back(places, attended, gattn, expert_in, glog):
    vmem = pl.BlockSpec(memory_space=pltpu.VMEM)
    return kernel_call(
        project_back_body,
        (struct((PAIRS, 64, D), BF16),) * 2 + (struct((D, LANE), F32),),
        flops=2 * ROWS * D * D,
        nbytes=6 * 2**20,
        in_specs=[pl.BlockSpec(memory_space=pltpu.SMEM)] + [vmem] * 4,
        scratch_shapes=[pltpu.VMEM((N_SHARD, 64, D), BF16)],
    )(places, attended, gattn, expert_in, glog)


def interleave(kv):
    return jnp.swapaxes(kv.reshape(-1, 2, KVH, HD), 1, 2).reshape(-1, D)


def separate(kv):
    return jnp.swapaxes(kv.reshape(-1, KVH, 2, HD), 1, 2).reshape(-1, D)


def spread(per_expert):
    rows = per_expert.shape[0]
    padded = jnp.pad(per_expert.reshape(rows, N_SHARD, 2), ((0, 0), (0, 0), (0, 6)))
    return padded.reshape(rows, LANE)


def rope_tables(ctx):
    half = HD // 2
    positions = ctx * BLK + jnp.arange(BLK, dtype=jnp.int32)
    frequency = ROPE_BASE ** (-2.0 * jnp.arange(half, dtype=F32) / HD)
    angles = positions.astype(F32)[:, None] * frequency[None, :]
    c, s = jnp.cos(angles), jnp.sin(angles)
    c, s = jnp.concatenate([c, c], axis=1), jnp.concatenate([-s, s], axis=1)
    one, zero = jnp.ones_like(c), jnp.zeros_like(c)
    pairs = [(c, c), (s, s), (c, one), (s, zero)]
    tables = jnp.stack([jnp.concatenate(p, axis=1) for p in pairs])
    return jnp.concatenate([tables] * SEQS, axis=1)


def to_every(own, axis):
    count = lax.axis_size(axis)
    copies = jnp.broadcast_to(own[None], (count,) + own.shape)
    return lax.all_to_all(copies, axis, 0, 0, tiled=True)


def with_other_core(keep, give):
    got = lax.ppermute(give, "shard", OTHER_CORE)
    return (keep.astype(F32) + got.astype(F32)).astype(BF16)


def local(
    hidden_in,
    routes,
    prefix,
    gain_attention,
    w_query,
    w_keyval,
    gain_query,
    gain_key,
    w_output,
    gain_experts,
    w_router,
    w_gate_up,
    w_down,
    cotangent,
):
    shard = lax.axis_index("shard")
    ctx = lax.axis_index("ctx")
    core = shard % 2
    x = hidden_in.reshape(ROWS, D)
    cot = cotangent.reshape(ROWS, D)

    key_rows = jnp.pad(gain_key, (0, 32))
    columns = jnp.stack([gain_attention, gain_query, key_rows, gain_experts], axis=1)
    first = lax.all_gather(
        jnp.concatenate(
            [w_query, interleave(w_keyval), spread(w_router), jnp.pad(columns, ((0, 0), (0, LANE - 4)))],
            axis=1,
        ),
        "shard",
        axis=0,
        tiled=True,
    )
    router = first[:, 2 * D : LAST]
    own_w = jnp.concatenate([w_gate_up, jnp.swapaxes(w_down, 1, 2)], axis=2)
    other_w = lax.ppermute(own_w, "ctx", X_HI)
    up, down, far = (lax.ppermute(own_w, "ctx", y_shift(step)) for step in (1, -1, 2))
    x, own_w, other_w, up, down, far = lax.optimization_barrier((x, own_w, other_w, up, down, far))
    high, low = ctx // 4 * 4, ctx % 4
    sources = []
    for step in (0, -1, 1, 2):
        sources += [high + (low + step) % 4, 4 - high + (low + step) % 4]
    places = jnp.stack([shard, *sources]).astype(jnp.int32)

    lanes = jnp.arange(LANE, dtype=jnp.int32)
    named = jnp.where(lanes % 8 < 2, lanes // 8 * 2 + lanes % 8, -1)
    member = jnp.any(routes.reshape(ROWS, -1)[:, :, None] == named, axis=1).astype(BF16)
    sent = jnp.concatenate([cot, member], axis=1)
    sent = jnp.concatenate([sent, jnp.pad(w_output, ((0, 0), (0, LANE)))])
    all_out = lax.all_gather(sent, "shard", axis=0)
    own_member = lax.dynamic_slice(all_out, (0, 0, D + 8 * shard), (N_SHARD, ROWS, 2))
    own_member = own_member.reshape(N_SHARD, SEQS, BLK, 2)
    earlier = jnp.tril(jnp.ones((BLK, BLK), BF16), -1)
    slots = jnp.einsum("ts,nbse->nebt", earlier, own_member, preferred_element_type=F32)
    slots = slots + jnp.arange(SEQS, dtype=F32)[:, None] * CAP
    slots = jnp.where(jnp.transpose(own_member, (0, 3, 1, 2)) > 0, slots, -1.0)
    slots = slots.reshape(PAIRS, 2, 2, ROWS)

    rope = rope_tables(ctx)
    packed, normed, q_raw, kv_raw, gains = front(x, first, rope)
    packed = lax.all_to_all(packed, "ctx", 0, 0, tiled=True)
    att = lax.all_to_all(attend(prefix, packed), "ctx", 0, 0, tiled=True)
    residual, attended, expert_in, wo = middle(x, att, all_out, gains)

    all_in = lax.all_gather(expert_in, "shard", axis=0)
    other, _ = lax.optimization_barrier((other_w, expert_in))
    other_up, other_down, other_far = (lax.ppermute(other, "ctx", y_shift(step)) for step in (1, -1, 2))
    back_keep, back_give, out, gg, rows_in, rows_grad, mid, dgu = experts(
        places,
        all_in.reshape(PAIRS, 2, ROWS, D),
        all_out.reshape(PAIRS, 2, ROWS + 64, D + LANE),
        slots,
        router,
        (own_w, other_w, up, other_up, down, other_down, far, other_far),
    )
    gg = lax.all_to_all(gg.reshape(N_SHARD, 8, ROWS), "shard", 0, 0, tiled=True)
    both = with_other_core(back_keep, back_give)
    both, gg, rows_in = lax.optimization_barrier((both, gg, rows_in))
    parts = lax.all_to_all(both, "shard", 0, 0, tiled=True, axis_index_groups=LANES)
    gw_own, gw_down, gw_up, gw_far = expert_grads(places, rows_in, rows_grad, mid, dgu)
    gw_down = lax.ppermute(gw_down, "ctx", y_shift(-1))
    gw_up = lax.ppermute(gw_up, "ctx", y_shift(1))
    gw_far = lax.ppermute(gw_far, "ctx", y_shift(2))
    parts, gw_up, gw_down = lax.optimization_barrier((parts, gw_up, gw_down))
    gatt, gres, gattn, glog, gain_e = turn(
        parts, gg, expert_in, residual, cot, member, router, gains, wo
    )

    gattn, out = lax.optimization_barrier((gattn, out))

    gatt = lax.all_to_all(gatt, "ctx", 0, 0, tiled=True)
    grads = lax.all_to_all(attend_back(prefix, packed, gatt), "ctx", 0, 0, tiled=True)
    grads, gw_far = lax.optimization_barrier((grads, gw_far))
    wo_keep, wo_give, beside = project_back(places, attended, gattn, expert_in, glog)
    grad_input, gw_keep, gw_give = finish(
        places, grads, q_raw, kv_raw, x, normed, gres, first, gains, rope, beside, gain_e
    )

    moe = lax.psum_scatter(
        out.reshape(N_SHARD, ROWS, D), "shard", scatter_dimension=0, tiled=True
    )
    layer_out = (residual + moe[0].astype(F32)).astype(BF16)

    pieces = sum(g.astype(F32) for g in (gw_own, gw_up, gw_down, gw_far)).astype(BF16)
    pieces = pieces[0].astype(F32) + lax.ppermute(pieces[1], "ctx", X_HI).astype(F32)
    dense = with_other_core(
        jnp.concatenate([gw_keep, wo_keep], axis=2), jnp.concatenate([gw_give, wo_give], axis=2)
    )
    dense = dense.reshape(PAIRS * N_CTX, 8, -1)
    dense = lax.all_to_all(dense, ("shard", "ctx"), 0, 0, tiled=True, axis_index_groups=CHIPS)
    dense = to_every(dense.astype(F32).sum(axis=0).astype(BF16), "ctx")
    dense = dense.reshape(64, -1).astype(F32)
    beside = dense[:, 2 * D : LAST]
    g_router = beside.reshape(64, N_SHARD, 8)[..., :2].reshape(64, E)
    return (
        layer_out.reshape(hidden_in.shape),
        grad_input.reshape(hidden_in.shape),
        beside[:, 2],
        dense[:, 0:D],
        separate(dense[:, D : 2 * D]),
        beside[:, 3],
        beside[0:32, 4],
        dense[:, LAST:],
        beside[:, 5],
        g_router,
        pieces[..., : 2 * FF],
        jnp.swapaxes(pieces[..., 2 * FF :], 1, 2),
    )


def solution(mesh):
    rows = P("shard", "ctx", None)
    flat, line = P("shard", None), P("shard")
    return jax.shard_map(
        local,
        mesh=mesh,
        in_specs=(rows, rows, line, line, flat, flat, line, line, flat, line, flat, rows, P("shard", None, "ctx"), rows),
        out_specs=(rows, rows, line, flat, flat, line, line, flat, line, flat, rows, P("shard", None, "ctx")),
        check_vma=False,
    )
```

time: 1030 us -> 553 us (0.54)
  waiting for transfers between devices: 449 us -> 234 us
  local copies, waits for them, and re-layouts: 200 us -> 36.4 us
  matrix products: 127 us -> 0.22 us
  Pallas kernels: 0 us -> 115 us
  other arithmetic: 96.4 us -> 27.5 us
  blocking collectives: 73.6 us -> 51 us
    all_to_all x12 -> x6, waiting for transfers between devices: 266 us -> 72.2 us  [the longest x1 49.7 us: local(): lax.all_to_all(dense, ('shard', 'ctx'), 0, 0, tiled=True, axis_index_grou...]
    dot_general x24 -> x1, matrix products: 127 us -> 0.22 us  [local(): jnp.einsum('ts,nbse->nebt', earlier, own_member, preferred_element_type=F32)]
    ppermute x0 -> x13, waiting for transfers between devices: none -> 117 us  [the longest x1 33.9 us: local(): gw_up = lax.ppermute(gw_up, 'ctx', y_shift(1))]
    pallas_call x0 -> x9, Pallas kernels: none -> 115 us  [the longest x1 48.4 us: experts(): kernel_call(experts_body, (struct((PAIRS, ROWS, D), BF16),) * 2 + (struct...]
    reduce_scatter x2 -> x1, waiting for transfers between devices: 109 us -> 0.01 us  [local(): lax.psum_scatter(out.reshape(N_SHARD, ROWS, D), 'shard', scatter_dimensio...]
    unnamed x2 -> x0, blocking collectives: 73.6 us -> none
    gather x4 -> x0, local copies, waits for them, and re-layouts: 61.8 us -> none  [the longest x1 18.6 us: local(): padded_grads[slot_table]]
    all_to_all x0 -> x2, blocking collectives: none -> 51 us  [the longest x1 31.6 us: local(): packed = lax.all_to_all(packed, 'ctx', 0, 0, tiled=True)]
  transfers between devices with their start and end apart: 20 -> 23, of which waited for: 16 -> 16; matrix products, arithmetic and copies ran while one was open for 30% -> 7% of each run, Pallas kernels for 0% -> 11%
where the time goes in v1:
time: 553 us; the launch traced here: 544 us
  waiting for transfers between devices  234 us (42%)
  Pallas kernels  115 us (21%)
  starting transfers between devices  65.8 us (12%)
  blocking collectives  51 us (9%)
  local copies, waits for them, and re-layouts  36.4 us (7%)
  other arithmetic  27.5 us (5%)
  between operations  14.6 us (3%)
    all_to_all x1, waiting for transfers between devices, local(): lax.all_to_all(dense, ('shard', 'ctx'), 0, 0, tiled=True, axis_index_grou...  49.7 us
    pallas_call x1, Pallas kernels, experts(): kernel_call(experts_body, (struct((PAIRS, ROWS, D), BF16),) * 2 + (struct...  48.4 us
    ppermute x1, waiting for transfers between devices, local(): gw_up = lax.ppermute(gw_up, 'ctx', y_shift(1))  33.9 us
    all_to_all x1, blocking collectives, local(): packed = lax.all_to_all(packed, 'ctx', 0, 0, tiled=True)  31.6 us
    ppermute x3, waiting for transfers between devices, local(): lax.ppermute(own_w, 'ctx', y_shift(step))  30.1 us
    ppermute x3, waiting for transfers between devices, local(): lax.ppermute(other, 'ctx', y_shift(step))  27.9 us
    all_gather x1, waiting for transfers between devices, local(): all_out = lax.all_gather(sent, 'shard', axis=0)  22.4 us
    unnamed x72, local copies, waits for them, and re-layouts  20.9 us
  transfers between devices with their start and end apart: 23, of which 16 were waited for; matrix products, arithmetic and copies ran while one was open for 7% of the time, Pallas kernels for 11%

profile of v1, /device:TPU:2, one launch (start us, length us, event | category | flops | bytes accessed | tf_op | source)
XLA Modules:
  0.0 544.1 jit_solution(7388584651715451861)
XLA Ops:
  24.7 13.9 %collective-permute-done.3.p6 = bf16[2,128,1536]{2,1,0:T(8,128)(2,1)S(1)} collective-permute-done((bf16[2,128,1536]{2,1,0:T(8,128)(2,1)S(1)}, bf16[2,128,1536]{2,1,0:T(8,128)(2,1)S(1)}, u32[]{:S(2)}, u32[]{:S(2)}) %collective-permute-start.3) | collective-permute-done | bytes 786464 | tf_op jit(solution)/shard_map/ppermute | solution.py:662
  38.6 16.1 %collective-permute-done.2.p4 = bf16[2,128,1536]{2,1,0:T(8,128)(2,1)} collective-permute-done((bf16[2,128,1536]{2,1,0:T(8,128)(2,1)S(1)}, bf16[2,128,1536]{2,1,0:T(8,128)(2,1)}, u32[]{:S(2)}, u32[]{:S(2)}) %collective-permute-start.2) | collective-permute-done | bytes 786464 | tf_op jit(solution)/shard_map/ppermute | solution.py:662
  58.8 6.8 %all-gather.6.cloned.1.call-done.w_ref = bf16[1024,2304]{1,0:T(8,128)(2,1)} async-done(((bf16[64,2304]{1,0:T(8,128)(2,1)}), bf16[1024,2304]{1,0:T(8,128)(2,1)}) %all-gather.6.cloned.1.call-update) | async-done | bytes 4718608 | tf_op jit(solution)/shard_map/all_gather | solution.py:650
  71.2 31.6 %all_to_all.40.in_ref = bf16[8,256,256]{2,1,0:T(8,128)(2,1)S(1)} all-to-all(bf16[8,256,256]{2,1,0:T(8,128)(2,1)S(1)} %get-tuple-element.62), channel_id=1, replica_groups=mesh['shard'=16,'ctx'=8] {'ctx'}, dimensions={0} | all-to-all | bytes 2097152 | tf_op jit(solution)/shard_map/all_to_all | solution.py:686
  102.8 7.4 %shard_map.230 = bf16[8,256,128]{2,1,0:T(8,128)(2,1)S(1)} custom-call(s32[2]{0:T(128)S(1)} %copy-done.27, bf16[8,256,256]{2,1,0:T(8,128)(2,1)S(1)} %all_to_all.40.in_ref), custom_call_target="tpu_custom_call" | custom-call | flops 1073741824 | bytes 2097152 | tf_op jit(solution)/shard_map/pallas_call | solution.py:185
  110.2 19.4 %all_to_all.41.att_ref = bf16[8,256,128]{2,1,0:T(8,128)(2,1)S(1)} all-to-all(bf16[8,256,128]{2,1,0:T(8,128)(2,1)S(1)} %shard_map.230), channel_id=1, replica_groups=mesh['shard'=16,'ctx'=8] {'ctx'}, dimensions={0} | all-to-all | bytes 1048576 | tf_op jit(solution)/shard_map/all_to_all | solution.py:687
  129.6 22.4 %all-gather.8.cloned.1.call-done = bf16[5120,1152]{1,0:T(8,128)(2,1)} async-done(((bf16[320,1152]{1,0:T(8,128)(2,1)}), bf16[5120,1152]{1,0:T(8,128)(2,1)}) %all-gather.8.cloned.1.call-update) | async-done | bytes 11796496 | tf_op jit(solution)/shard_map/all_gather | solution.py:675
  168.4 11.4 %collective-permute-done.6.p7 = bf16[2,128,1536]{2,1,0:T(8,128)(2,1)} collective-permute-done((bf16[2,128,1536]{2,1,0:T(8,128)(2,1)}, bf16[2,128,1536]{2,1,0:T(8,128)(2,1)}, u32[]{:S(2)}, u32[]{:S(2)}) %collective-permute-start.6) | collective-permute-done | bytes 786464 | tf_op jit(solution)/shard_map/ppermute | solution.py:692
  179.8 16.5 %collective-permute-done.5.p5 = bf16[2,128,1536]{2,1,0:T(8,128)(2,1)} collective-permute-done((bf16[2,128,1536]{2,1,0:T(8,128)(2,1)}, bf16[2,128,1536]{2,1,0:T(8,128)(2,1)}, u32[]{:S(2)}, u32[]{:S(2)}) %collective-permute-start.5) | collective-permute-done | bytes 786464 | tf_op jit(solution)/shard_map/ppermute | solution.py:692
  196.3 15.6 %all-gather.10.cloned.1.call-done = bf16[4096,1024]{1,0:T(8,128)(2,1)} async-done(((bf16[256,1024]{1,0:T(8,128)(2,1)}), bf16[4096,1024]{1,0:T(8,128)(2,1)}) %all-gather.10.cloned.1.call-update) | async-done | bytes 8388624 | tf_op jit(solution)/shard_map/all_gather | solution.py:690
  211.9 48.4 %shard_map.232 = (bf16[8,256,1024]{2,1,0:T(8,128)(2,1)}, bf16[8,256,1024]{2,1,0:T(8,128)(2,1)}, bf16[8,2,256,1024]{3,2,1,0:T(8,128)(2,1)}, f32[8,2,8,256]{3,2,1,...) custom-call(s32[9]{0:T(128)} %stack.79.me_ref, ...), custom_call_target="tpu_custom_call" | custom-call | flops 30000001024 | bytes 62914560 | tf_op jit(solution)/shard_map/pallas_call | solution.py:386
  260.7 16.2 %all-to-all-start.2 = ((f32[16,8,256]{2,1,0:T(8,128)}), f32[16,8,256]{2,1,0:T(8,128)S(1)}, u32[]{:S(2)}, u32[]{:S(2)}) async-start(f32[16,8,256]{2,1,0:T(8,128)} %bitcast.88), calls=%async_computation.2 | async-start | bytes 262144 | tf_op jit(solution)/shard_map/all_to_all | solution.py:701
  276.9 7.7 %add_convert_fusion = bf16[8,256,1024]{2,1,0:T(8,128)(2,1)} fusion(bf16[8,256,1024]{2,1,0:T(8,128)(2,1)} %collective-permute-done.7, bf16[8,256,1024]{2,1,0:T(8,128)(2,1)} %get-tuple-element.72), kind=kLoop, calls=%fused_computation | loop fusion | flops 8388608 | bytes 12582912 | tf_op jit(solution)/shard_map/convert_element_type | solution.py:623
  284.7 5.8 %all-to-all-start.3 = ((bf16[8,256,1024]{2,1,0:T(8,128)(2,1)}), bf16[8,256,1024]{2,1,0:T(8,128)(2,1)}, u32[]{:S(2)}, u32[]{:S(2)}) async-start(bf16[8,256,1024]{2,1,0:T(8,128)(2,1)} %add_convert_fusion), calls=%async_computation.3 | async-start | bytes 8388608 | tf_op jit(solution)/shard_map/all_to_all | solution.py:704
  290.5 18.1 %shard_map.233 = (bf16[2,2,128,1536]{3,2,1,0:T(8,128)(2,1)S(1)}, bf16[2,2,128,1536]{3,2,1,0:T(8,128)(2,1)S(1)}, bf16[2,2,128,1536]{3,2,1,0:T(8,128)(2,1)S(1)}, bf16[2,2,128,1536]{3,2,1,0:T(8,128)(2,1)}) custom-call(s32[9]{0:T(128)S(1)} %copy-done.22, bf16[2,1536,1024]{2,1,0:T(8,128)(2,1)} %get-tuple-element.77.xa_ref.xb_ref, ...), custom_call_target="tpu_custom_call" | custom-call | flops 9663676416 | bytes 31457280 | tf_op jit(solution)/shard_map/pallas_call | solution.py:448
  313.1 33.9 %collective-permute-done.8 = bf16[2,2,128,1536]{3,2,1,0:T(8,128)(2,1)S(1)} collective-permute-done((bf16[2,2,128,1536]{3,2,1,0:T(8,128)(2,1)S(1)}, bf16[2,2,128,1536]{3,2,1,0:T(8,128)(2,1)S(1)}, u32[]{:S(2)}, u32[]{:S(2)}) %collective-permute-start.8) | collective-permute-done | bytes 1572896 | tf_op jit(solution)/shard_map/ppermute | solution.py:707
  364.4 9.3 %all-to-all-done.4.grad_ref = bf16[8,256,128]{2,1,0:T(8,128)(2,1)} async-done(((bf16[8,256,128]{2,1,0:T(8,128)(2,1)}), bf16[8,256,128]{2,1,0:T(8,128)(2,1)}, u32[]{:S(2)}, u32[]{:S(2)}) %all-to-all-start.4) | async-done | bytes 524320 | tf_op jit(solution)/shard_map/all_to_all | solution.py:716
  373.8 14.6 %shard_map.235 = bf16[8,256,256]{2,1,0:T(8,128)(2,1)S(1)} custom-call(s32[2]{0:T(128)S(1)} %copy-done.27, bf16[8,256,256]{2,1,0:T(8,128)(2,1)S(1)} %copy-done.15, bf16[8,256,128]{2,1,0:T(8,128)(2,1)} %all-to-all-done.4.grad_ref), custom_call_target="tpu_custom_call" | custom-call | flops 2684354560 | bytes 3145728 | tf_op jit(solution)/shard_map/pallas_call | solution.py:244
  401.1 7.0 %collective-permute-done.10 = bf16[2,2,128,1536]{3,2,1,0:T(8,128)(2,1)} collective-permute-done((bf16[2,2,128,1536]{3,2,1,0:T(8,128)(2,1)}, bf16[2,2,128,1536]{3,2,1,0:T(8,128)(2,1)}, u32[]{:S(2)}, u32[]{:S(2)}) %collective-permute-start.10) | collective-permute-done | bytes 1572896 | tf_op jit(solution)/shard_map/ppermute | solution.py:708
  408.1 11.5 %all-to-all-done.5.rows_ref = bf16[8,256,256]{2,1,0:T(8,128)(2,1)S(1)} async-done(((bf16[8,256,256]{2,1,0:T(8,128)(2,1)}), bf16[8,256,256]{2,1,0:T(8,128)(2,1)S(1)}, u32[]{:S(2)}, u32[]{:S(2)}) %all-to-all-start.5) | async-done | bytes 1048608 | tf_op jit(solution)/shard_map/all_to_all | solution.py:717
  424.2 10.5 %shard_map.237 = (bf16[256,1024]{1,0:T(8,128)(2,1)}, bf16[8,64,2176]{2,1,0:T(8,128)(2,1)}, bf16[8,64,2176]{2,1,0:T(8,128)(2,1)}) custom-call(s32[9]{0:T(128)S(1)} %copy-done.22, bf16[8,256,256]{2,1,0:T(8,128)(2,1)S(1)} %all-to-all-done.5.rows_ref, f32[256,1024]{1,0:T(8,128)S(1)} %copy-done.5, f32[256,1024]{1,0:T(8,128)S(1)} %copy-done.7, ...), custom_call_target="tpu_custom_call" | custom-call | flops 2147483648 | bytes 15728640 | tf_op jit(solution)/shard_map/pallas_call | solution.py:551
  445.2 8.5 %all-to-all-start.6 = ((bf16[64,8,3200]{2,1,0:T(8,128)(2,1)}), bf16[64,8,3200]{2,1,0:T(8,128)(2,1)}, u32[]{:S(2)}, u32[]{:S(2)}) async-start(bf16[64,8,3200]{2,1,0:T(8,128)(2,1)} %bitcast.81), calls=%async_computation.7 | async-start | bytes 6553600 | tf_op jit(solution)/shard_map/all_to_all | solution.py:735
  460.9 49.7 %all-to-all-done.6 = bf16[64,8,3200]{2,1,0:T(8,128)(2,1)} async-done(((bf16[64,8,3200]{2,1,0:T(8,128)(2,1)}), bf16[64,8,3200]{2,1,0:T(8,128)(2,1)}, u32[]{:S(2)}, u32[]{:S(2)}) %all-to-all-start.6) | async-done | bytes 3276832 | tf_op jit(solution)/shard_map/all_to_all | solution.py:735
  517.2 8.2 %collective-permute-done.12 = bf16[2,128,1536]{2,1,0:T(8,128)(2,1)} collective-permute-done((bf16[2,128,1536]{2,1,0:T(8,128)(2,1)S(1)}, bf16[2,128,1536]{2,1,0:T(8,128)(2,1)}, u32[]{:S(2)}, u32[]{:S(2)}) %collective-permute-start.12) | collective-permute-done | bytes 786464 | tf_op jit(solution)/shard_map/ppermute | solution.py:730
  (163 shorter events, 118.8 us)
Async XLA Ops:
  7.2 58.4 %all-gather.6.cloned.1.call-start = ((), (), s32[]{:S(2)}) async-start(), calls=%async_computation.9 | async-start | bytes 5013504 | tf_op jit(solution)/shard_map/all_gather | solution.py:650
  12.8 139.1 %all-gather.8.cloned.1.call-start = ((), (), s32[]{:S(2)}) async-start(), calls=%async_computation.11 | async-start | bytes 12533760 | tf_op jit(solution)/shard_map/all_gather | solution.py:675
  16.3 195.7 %all-gather.10.cloned.1.call-start = ((), (), s32[]{:S(2)}) async-start(), calls=%async_computation.12 | async-start | bytes 8912896 | tf_op jit(solution)/shard_map/all_gather | solution.py:690
  16.6 22.1 %collective-permute-start.3 = (bf16[2,128,1536]{2,1,0:T(8,128)(2,1)S(1)}, bf16[2,128,1536]{2,1,0:T(8,128)(2,1)S(1)}, u32[]{:S(2)}, u32[]{:S(2)}) collective-permute-start(bf16[2,128,1536]{2,1,0:T(8,128)(2,1)S(1)} %pad_maximum_fusion.1.p0), channel_id=1, source_target_pairs={{0,2},{1,3},{2,0},{3,1},{4,6},{5,7},{6,4},{7,5},{8,10},{9,11},{10,... | collective-permute-start | bytes 2359304 | tf_op jit(solution)/shard_map/ppermute | solution.py:662
  19.8 34.9 %collective-permute-start.2 = (bf16[2,128,1536]{2,1,0:T(8,128)(2,1)S(1)}, bf16[2,128,1536]{2,1,0:T(8,128)(2,1)}, u32[]{:S(2)}, u32[]{:S(2)}) collective-permute-start(bf16[2,128,1536]{2,1,0:T(8,128)(2,1)S(1)} %pad_maximum_fusion.1.p0), channel_id=1, source_target_pairs={{0,3},{1,0},{2,1},{3,2},{4,7},{5,4},{6,5},{7,6},{8,11},{9,8},{10,9... | collective-permute-start | bytes 2359304 | tf_op jit(solution)/shard_map/ppermute | solution.py:662
  20.9 33.9 %collective-permute-start.1 = (bf16[2,128,1536]{2,1,0:T(8,128)(2,1)S(1)}, bf16[2,128,1536]{2,1,0:T(8,128)(2,1)}, u32[]{:S(2)}, u32[]{:S(2)}) collective-permute-start(bf16[2,128,1536]{2,1,0:T(8,128)(2,1)S(1)} %pad_maximum_fusion.1.p0), channel_id=1, source_target_pairs={{0,1},{1,2},{2,3},{3,0},{4,5},{5,6},{6,7},{7,4},{8,9},{9,10},{10,1... | collective-permute-start | bytes 2359304 | tf_op jit(solution)/shard_map/ppermute | solution.py:662
  21.9 36.9 %collective-permute-start = (bf16[2,128,1536]{2,1,0:T(8,128)(2,1)S(1)}, bf16[2,128,1536]{2,1,0:T(8,128)(2,1)}, u32[]{:S(2)}, u32[]{:S(2)}) collective-permute-start(bf16[2,128,1536]{2,1,0:T(8,128)(2,1)S(1)} %pad_maximum_fusion.1.p0), channel_id=1, source_target_pairs={{0,4},{1,5},{2,6},{3,7},{4,0},{5,1},{6,2},{7,3},{8,12},{9,13},{10,... | collective-permute-start | bytes 2359304 | tf_op jit(solution)/shard_map/ppermute | solution.py:661
  38.6 64.2 %copy-start.34 = (bf16[2,128,1536]{2,1,0:T(8,128)(2,1)}, bf16[2,128,1536]{2,1,0:T(8,128)(2,1)S(1)}, u32[]{:S(2)}) copy-start(bf16[2,128,1536]{2,1,0:T(8,128)(2,1)S(1)} %collective-permute-done.3.p6) | copy-start | bytes 2359300
  157.5 22.3 %collective-permute-start.6 = (bf16[2,128,1536]{2,1,0:T(8,128)(2,1)}, bf16[2,128,1536]{2,1,0:T(8,128)(2,1)}, u32[]{:S(2)}, u32[]{:S(2)}) collective-permute-start(bf16[2,128,1536]{2,1,0:T(8,128)(2,1)} %collective-permute-done.p1), channel_id=1, source_target_pairs={{0,2},{1,3},{2,0},{3,1},{4,6},{5,7},{6,4},{7,5},{8,10},{9,11},{10,... | collective-permute-start | bytes 2359304 | tf_op jit(solution)/shard_map/ppermute | solution.py:692
  160.9 35.4 %collective-permute-start.5 = (bf16[2,128,1536]{2,1,0:T(8,128)(2,1)}, bf16[2,128,1536]{2,1,0:T(8,128)(2,1)}, u32[]{:S(2)}, u32[]{:S(2)}) collective-permute-start(bf16[2,128,1536]{2,1,0:T(8,128)(2,1)} %collective-permute-done.p1), channel_id=1, source_target_pairs={{0,3},{1,0},{2,1},{3,2},{4,7},{5,4},{6,5},{7,6},{8,11},{9,8},{10,9... | collective-permute-start | bytes 2359304 | tf_op jit(solution)/shard_map/ppermute | solution.py:692
  162.0 34.3 %collective-permute-start.4 = (bf16[2,128,1536]{2,1,0:T(8,128)(2,1)}, bf16[2,128,1536]{2,1,0:T(8,128)(2,1)}, u32[]{:S(2)}, u32[]{:S(2)}) collective-permute-start(bf16[2,128,1536]{2,1,0:T(8,128)(2,1)} %collective-permute-done.p1), channel_id=1, source_target_pairs={{0,1},{1,2},{2,3},{3,0},{4,5},{5,6},{6,7},{7,4},{8,9},{9,10},{10,1... | collective-permute-start | bytes 2359304 | tf_op jit(solution)/shard_map/ppermute | solution.py:692
  260.4 16.6 %collective-permute-start.7 = (bf16[8,256,1024]{2,1,0:T(8,128)(2,1)}, bf16[8,256,1024]{2,1,0:T(8,128)(2,1)}, u32[]{:S(2)}, u32[]{:S(2)}) collective-permute-start(bf16[8,256,1024]{2,1,0:T(8,128)(2,1)} %get-tuple-element.73), channel_id=1, source_target_pairs={{0,8},{8,0},{16,24},{24,16},{32,40},{40,32},{48,56},{56,48},{64,72... | collective-permute-start | bytes 12582920 | tf_op jit(solution)/shard_map/ppermute | solution.py:622
  260.7 24.0 %all-to-all-start.2 = ((f32[16,8,256]{2,1,0:T(8,128)}), f32[16,8,256]{2,1,0:T(8,128)S(1)}, u32[]{:S(2)}, u32[]{:S(2)}) async-start(f32[16,8,256]{2,1,0:T(8,128)} %bitcast.88), calls=%async_computation.2 | async-start | bytes 262144 | tf_op jit(solution)/shard_map/all_to_all | solution.py:701
  284.7 63.4 %all-to-all-start.3 = ((bf16[8,256,1024]{2,1,0:T(8,128)(2,1)}), bf16[8,256,1024]{2,1,0:T(8,128)(2,1)}, u32[]{:S(2)}, u32[]{:S(2)}) async-start(bf16[8,256,1024]{2,1,0:T(8,128)(2,1)} %add_convert_fusion), calls=%async_computation.3 | async-start | bytes 8388608 | tf_op jit(solution)/shard_map/all_to_all | solution.py:704
  290.5 244.7 %reduce-scatter.2.cloned.1.call-start = ((), (), s32[]{:S(2)}) async-start(), calls=%async_computation.10 | async-start | bytes 8912896 | tf_op jit(solution)/shard_map/reduce_scatter | solution.py:724
  309.8 37.1 %collective-permute-start.8 = (bf16[2,2,128,1536]{3,2,1,0:T(8,128)(2,1)S(1)}, bf16[2,2,128,1536]{3,2,1,0:T(8,128)(2,1)S(1)}, u32[]{:S(2)}, u32[]{:S(2)}) collective-permute-start(bf16[2,2,128,1536]{3,2,1,0:T(8,128)(2,1)S(1)} %get-tuple-element.81), channel_id=1, source_target_pairs={{0,1},{1,2},{2,3},{3,0},{4,5},{5,6},{6,7},{7,4},{8,9},{9,10},{10,1... | collective-permute-start | bytes 4718600 | tf_op jit(solution)/shard_map/ppermute | solution.py:707
  311.3 36.7 %collective-permute-start.9 = (bf16[2,2,128,1536]{3,2,1,0:T(8,128)(2,1)S(1)}, bf16[2,2,128,1536]{3,2,1,0:T(8,128)(2,1)}, u32[]{:S(2)}, u32[]{:S(2)}) collective-permute-start(bf16[2,2,128,1536]{3,2,1,0:T(8,128)(2,1)S(1)} %get-tuple-element.82), channel_id=1, source_target_pairs={{0,3},{1,0},{2,1},{3,2},{4,7},{5,4},{6,5},{7,6},{8,11},{9,8},{10,9... | collective-permute-start | bytes 4718600 | tf_op jit(solution)/shard_map/ppermute | solution.py:706
  356.1 17.7 %all-to-all-start.4 = ((bf16[8,256,128]{2,1,0:T(8,128)(2,1)}), bf16[8,256,128]{2,1,0:T(8,128)(2,1)}, u32[]{:S(2)}, u32[]{:S(2)}) async-start(bf16[8,256,128]{2,1,0:T(8,128)(2,1)} %copy-done.21), calls=%async_computation.5 | async-start | bytes 1048576 | tf_op jit(solution)/shard_map/all_to_all | solution.py:716
  360.9 47.2 %collective-permute-start.10 = (bf16[2,2,128,1536]{3,2,1,0:T(8,128)(2,1)}, bf16[2,2,128,1536]{3,2,1,0:T(8,128)(2,1)}, u32[]{:S(2)}, u32[]{:S(2)}) collective-permute-start(bf16[2,2,128,1536]{3,2,1,0:T(8,128)(2,1)} %get-tuple-element.90), channel_id=1, source_target_pairs={{0,2},{1,3},{2,0},{3,1},{4,6},{5,7},{6,4},{7,5},{8,10},{9,11},{10,... | collective-permute-start | bytes 4718600 | tf_op jit(solution)/shard_map/ppermute | solution.py:708
  389.4 30.2 %all-to-all-start.5 = ((bf16[8,256,256]{2,1,0:T(8,128)(2,1)}), bf16[8,256,256]{2,1,0:T(8,128)(2,1)S(1)}, u32[]{:S(2)}, u32[]{:S(2)}) async-start(bf16[8,256,256]{2,1,0:T(8,128)(2,1)} %copy-done.16), calls=%async_computation.6 | async-start | bytes 2097152 | tf_op jit(solution)/shard_map/all_to_all | solution.py:717
  436.7 5.9 %collective-permute-start.11 = (bf16[8,64,3200]{2,1,0:T(8,128)(2,1)S(1)}, bf16[8,64,3200]{2,1,0:T(8,128)(2,1)S(1)}, u32[]{:S(2)}, u32[]{:S(2)}) collective-permute-start(bf16[8,64,3200]{2,1,0:T(8,128)(2,1)S(1)} %pad_maximum_fusion), channel_id=1, source_target_pairs={{0,8},{8,0},{16,24},{24,16},{32,40},{40,32},{48,56},{56,48},{64,72... | collective-permute-start | bytes 9830408 | tf_op jit(solution)/shard_map/ppermute | solution.py:622
  445.2 65.4 %all-to-all-start.6 = ((bf16[64,8,3200]{2,1,0:T(8,128)(2,1)}), bf16[64,8,3200]{2,1,0:T(8,128)(2,1)}, u32[]{:S(2)}, u32[]{:S(2)}) async-start(bf16[64,8,3200]{2,1,0:T(8,128)(2,1)} %bitcast.81), calls=%async_computation.7 | async-start | bytes 6553600 | tf_op jit(solution)/shard_map/all_to_all | solution.py:735
  458.8 66.7 %collective-permute-start.12 = (bf16[2,128,1536]{2,1,0:T(8,128)(2,1)S(1)}, bf16[2,128,1536]{2,1,0:T(8,128)(2,1)}, u32[]{:S(2)}, u32[]{:S(2)}) collective-permute-start(bf16[2,128,1536]{2,1,0:T(8,128)(2,1)S(1)} %slice_bitcast_fusion), channel_id=1, source_target_pairs={{0,4},{1,5},{2,6},{3,7},{4,0},{5,1},{6,2},{7,3},{8,12},{9,13},{10,... | collective-permute-start | bytes 2359304 | tf_op jit(solution)/shard_map/ppermute | solution.py:730
  513.8 17.1 %all-to-all-start.7 = ((bf16[8,8,3200]{2,1,0:T(8,128)(2,1)}), bf16[8,8,3200]{2,1,0:T(8,128)(2,1)S(1)}, u32[]{:S(2)}, u32[]{:S(2)}) async-start(bf16[8,8,3200]{2,1,0:T(8,128)(2,1)} %broadcast_in_dim.35), calls=%async_computation.8 | async-start | bytes 819200 | tf_op jit(solution)/shard_map/all_to_all | solution.py:618
  (34 other events, 462.3 us)
Sparse Core Ops, SparseCore 0:
  12.9 52.6 all-gather.5
  67.3 84.6 all-gather.7
  157.6 54.2 all-gather.9
  356.2 114.3 reduce-scatter.1
